TPU v7x, 32 devices: a whole 2x2x4 slice. The times are simulated.
32 devices in a mesh: row: 8 (over z, x), col: 4 (over y, core).
Axes of the slice: x: 2, y: 2, z: 4, core: 2. Of those that a mesh axis runs over, the one named last changes fastest.
Arguments:
- right_side: float32 [16, 512, 512], P(None, 'row', 'col'), may hold values from -8 to 8
- guess: float32 [16, 512, 512], P(None, 'row', 'col'), may hold values from -8 to 8
- material: int32 [16, 512, 512], P(None, 'row', 'col'), may hold values from 0 to 7
- conductivity: float32 [8], replicated, may hold values from 0.5 to 8
- capacity: float32 [8], replicated, may hold values from 0.004 to 0.1
Outputs:
- temperature: float32 [16, 512, 512], P(None, 'row', 'col')
- residual: float32 [16, 512, 512], P(None, 'row', 'col')
All inputs are finite; a program needn't handle non-finite values.
Results may differ from a plain program's by a relative error of at most 0.000042.
Values sent between devices are 32-bit elements; how exact they have to be, the bound alone decides.
A program may use at most 64 MiB of HBM per device.

v0:
```python
import jax
import jax.numpy as jnp
from jax import lax
from jax.sharding import PartitionSpec as P

COARSEN = 16
PRE = 2
POST = 2
CSWEEPS = 8


OMEGA = 0.8


def padded_2(cells, sides, width):
    for axis, dim in sides:
        count = lax.axis_size(axis)
        ends = count - 1
        head = lax.slice_in_dim(cells, 0, width, axis=dim)
        tail = lax.slice_in_dim(cells, cells.shape[dim] - width, cells.shape[dim], axis=dim)
        cells = jnp.concatenate(
            [
                lax.ppermute(tail, axis, [(i, (i + 1) % count) for i in range(ends)]),
                cells,
                lax.ppermute(head, axis, [((i + 1) % count, i) for i in range(ends)]),
            ],
            axis=dim,
        )
    return cells


def shifted(padded):
    return [
        padded[2:, 1:-1, 1:-1],
        padded[:-2, 1:-1, 1:-1],
        padded[1:-1, 2:, 1:-1],
        padded[1:-1, :-2, 1:-1],
        padded[1:-1, 1:-1, 2:],
        padded[1:-1, 1:-1, :-2],
    ]


def coefs_from(kap, padded, zfactor):
    coefs = []
    for index, other in enumerate(shifted(padded)):
        coef = 0.5 * (kap + other)
        if index < 2:
            coef = coef * zfactor
        coefs.append(coef)
    return coefs


def pad_depth(values):
    return jnp.pad(values, ((1, 1), (0, 0), (0, 0)))


def fine_pad(field):
    padded = padded_2(field, (("row", 1), ("col", 2)), 1)
    return pad_depth(padded)


def fine_apply(field, coefs, cap):
    result = cap * field
    for coef, other in zip(coefs, shifted(fine_pad(field))):
        result = result + coef * (field - other)
    return result


def thomas(diag_line, upper, rhs):
    depth = rhs.shape[0]
    gains = []
    heads = []
    denom = diag_line[0]
    gains.append(upper[0] / denom)
    heads.append(rhs[0] / denom)
    for level in range(1, depth):
        denom = diag_line[level] - upper[level - 1] * gains[level - 1]
        gains.append(upper[level] / denom)
        heads.append((rhs[level] + upper[level - 1] * heads[level - 1]) / denom)
    values = [None] * depth
    values[depth - 1] = heads[depth - 1]
    for level in range(depth - 2, -1, -1):
        values[level] = heads[level] + gains[level] * values[level + 1]
    return jnp.stack(values, axis=0)


def pad_rest(padded_x):
    return jnp.pad(padded_x, ((1, 1), (0, 0), (1, 1)))


def coarse_solve(coarse_res, kbar, kbar_x, capc, pad_rows):
    ccoefs = coefs_from(kbar, pad_rest(kbar_x), float(COARSEN * COARSEN))
    dcoarse = capc
    for coef in ccoefs:
        dcoarse = dcoarse + coef
    upper = ccoefs[0].at[-1].set(0.0)
    correction = jnp.zeros_like(coarse_res)
    for sweep in range(CSWEEPS):
        others = shifted(pad_rest(pad_rows(correction)))
        rhs = coarse_res
        for index in range(2, 6):
            rhs = rhs + ccoefs[index] * others[index]
        correction = thomas(dcoarse, upper, rhs)
    return correction


def shards(right_side, guess, material, conductivity, capacity):
    kappa = jnp.zeros(right_side.shape, jnp.float32)
    cap = jnp.zeros(right_side.shape, jnp.float32)
    for klass in range(conductivity.shape[0]):
        chosen = material == klass
        kappa = jnp.where(chosen, conductivity[klass], kappa)
        cap = jnp.where(chosen, capacity[klass], cap)
    depth, width_x, width_y = right_side.shape
    kappa_rim = padded_2(kappa, (("row", 1), ("col", 2)), 1)
    coefs = coefs_from(kappa, pad_depth(kappa_rim), 1.0)
    diag = cap
    for coef in coefs:
        diag = diag + coef

    def smooth(start, count):
        field = start
        for sweep in range(count):
            field = field + OMEGA * (right_side - fine_apply(field, coefs, cap)) / diag
        return (field, right_side - fine_apply(field, coefs, cap))

    field, fine_res = smooth(guess, PRE)
    cells_x = width_x // COARSEN
    cells_y = width_y // COARSEN
    shape_c = (depth, cells_x, COARSEN, cells_y, COARSEN)
    coarse_res = fine_res.reshape(shape_c).sum(axis=(2, 4))
    kbar = kappa.reshape(shape_c).sum(axis=(2, 4)) / (COARSEN * COARSEN)
    capc = cap.reshape(shape_c).sum(axis=(2, 4))
    strip_res, strip_kbar, strip_cap = (
        lax.all_gather(coarse_res, "col", axis=2, tiled=True),
        lax.all_gather(kbar, "col", axis=2, tiled=True),
        lax.all_gather(capc, "col", axis=2, tiled=True),
    )
    col_start = lax.axis_index("col") * cells_y
    kbar_x = padded_2(strip_kbar, (("row", 1),), 1)

    def rows_halo(values):
        return padded_2(values, (("row", 1),), 1)

    strip_corr = coarse_solve(strip_res, strip_kbar, kbar_x, strip_cap, rows_halo)
    correction = lax.dynamic_slice_in_dim(strip_corr, col_start, cells_y, 2)
    wide = jnp.broadcast_to(correction[:, :, None, :, None], shape_c).reshape(fine_res.shape)
    field, residual = smooth(field + wide, POST)
    return (field, residual)


def solution(mesh):
    placed = (P(None, "row", "col"), P(None, "row", "col"), P(None, "row", "col"), P(), P())
    return jax.shard_map(
        shards,
        mesh=mesh,
        in_specs=placed,
        out_specs=(P(None, "row", "col"), P(None, "row", "col")),
        check_vma=False,
    )
```

profile of v0, /device:TPU:0, one launch (start us, length us, event | category | flops | bytes accessed | tf_op | source)
XLA Modules:
  0.0 293.8 jit_solution(12412572603877755220)
XLA Ops:
  0.6 1.6 fusion.452
  2.3 7.5 %select_select_fusion = (f32[16,64,128]{2,1,0:T(8,128)S(1)}, pred[16,64,128]{2,1,0:T(8,128)(4,1)S(1)}, pred[16,64,128]{2,1,0:T(8,128)(4,1)S(1)}, pred[16,64,128]...) fusion(f32[]{:T(128)} %bitcast.15, f32[]{:T(128)} %bitcast.14, ...), kind=kLoop, calls=%fused_computation.233 | loop fusion | flops 2097152 | bytes 2097184 | tf_op jit(solution)/shard_map/jit(_where)/select_n | solution.py:112
  9.8 4.8 %collective-permute-start = (f32[16,1,128]{2,1,0:T(1,128)S(1)}, f32[16,1,128]{2,1,0:T(1,128)S(1)}, u32[]{:S(2)}, u32[]{:S(2)}) collective-permute-start(f32[16,1,128]{2,1,0:T(1,128)S(1)} %get-tuple-element.272), channel_id=1, source_target_pairs={{0,4},{4,8},{8,12},{12,16},{16,20},{20,24},{24,28},{1,5},{5,9},{9,... | collective-permute-start | bytes 24584 | tf_op jit(solution)/shard_map/ppermute | solution.py:23
  16.0 4.5 %collective-permute-start.4 = (f32[16,1,128]{2,1,0:T(1,128)S(1)}, f32[16,1,128]{2,1,0:T(1,128)S(1)}, u32[]{:S(2)}, u32[]{:S(2)}) collective-permute-start(f32[16,1,128]{2,1,0:T(1,128)S(1)} %get-tuple-element.274), channel_id=1, source_target_pairs={{0,4},{4,8},{8,12},{12,16},{16,20},{20,24},{24,28},{1,5},{5,9},{9,... | collective-permute-start | bytes 24584 | tf_op jit(solution)/shard_map/ppermute | solution.py:23
  27.7 4.8 %collective-permute-start.6 = (f32[16,66,1]{1,0,2:T(8,128)S(1)}, f32[16,66,1]{1,0,2:T(8,128)S(1)}, u32[]{:S(2)}, u32[]{:S(2)}) collective-permute-start(f32[16,66,1]{1,0,2:T(8,128)S(1)} %copy.259), channel_id=1, source_target_pairs={{0,1},{1,2},{2,3},{4,5},{5,6},{6,7},{8,9},{9,10},{10,11},{12,13},{... | collective-permute-start | bytes 12680 | tf_op jit(solution)/shard_map/ppermute | solution.py:23
  34.7 2.6 reshape.45
  37.3 2.6 reduce_sum.28
  40.0 5.6 %collective-permute-start.19 = (f32[16,1,32]{2,1,0:T(1,128)}, f32[16,1,32]{2,1,0:T(1,128)S(1)}, u32[]{:S(2)}, u32[]{:S(2)}) collective-permute-start(f32[16,1,32]{2,1,0:T(1,128)} %broadcast.79), channel_id=1, source_target_pairs={{0,4},{4,8},{8,12},{12,16},{16,20},{20,24},{24,28},{1,5},{5,9},{9,... | collective-permute-start | bytes 6152 | tf_op jit(solution)/shard_map/ppermute | solution.py:23
  49.6 9.4 %fusion.101 = (f32[16,64,128]{2,1,0:T(8,128)S(1)}, f32[16,64,128]{2,1,0:T(8,128)S(1)}, f32[16,64,128]{2,1,0:T(8,128)S(1)}, f32[16,64,128]{2,1,0:T(8,128)S(1)}, f...) fusion(f32[16,64,128]{2,1,0:T(8,128)S(1)} %copy-done.32, f32[16,64,128]{2,1,0:T(8,128)S(1)} %copy-done, ...), kind=kLoop, calls=%fused_computation.189 | loop fusion | flops 8519680 | bytes 7914016 | tf_op jit(solution)/shard_map/add | solution.py:124
  59.8 4.8 %collective-permute-start.8 = (f32[16,1,128]{2,1,0:T(1,128)S(1)}, f32[16,1,128]{2,1,0:T(1,128)S(1)}, u32[]{:S(2)}, u32[]{:S(2)}) collective-permute-start(f32[16,1,128]{2,1,0:T(1,128)S(1)} %get-tuple-element.270), channel_id=1, source_target_pairs={{0,4},{4,8},{8,12},{12,16},{16,20},{20,24},{24,28},{1,5},{5,9},{9,... | collective-permute-start | bytes 24584 | tf_op jit(solution)/shard_map/ppermute | solution.py:23
  65.9 7.2 %all_gather.10 = f32[16,4,32]{0,1,2:T(4,128)S(1)} all-gather(f32[16,4,8]{0,1,2:T(4,128)S(1)} %copy.281), channel_id=1, replica_groups=mesh['row'=8,'col'=4] {'col'}, dimensions={2}, use_global_device_ids=true | all-gather | bytes 10240 | tf_op jit(solution)/shard_map/all_gather | solution.py:136
  76.8 2.3 collective-permute-start.10
  83.1 5.2 %collective-permute-start.18 = (f32[16,1,32]{2,1,0:T(1,128)S(1)}, f32[16,1,32]{2,1,0:T(1,128)S(1)}, u32[]{:S(2)}, u32[]{:S(2)}) collective-permute-start(f32[16,1,32]{2,1,0:T(1,128)S(1)} %get-tuple-element.292), channel_id=1, source_target_pairs={{0,4},{4,8},{8,12},{12,16},{16,20},{20,24},{24,28},{1,5},{5,9},{9,... | collective-permute-start | bytes 6152 | tf_op jit(solution)/shard_map/ppermute | solution.py:23
  90.5 2.1 select_maximum_fusion.16
  94.0 4.8 %collective-permute-start.12 = (f32[16,1,128]{2,1,0:T(1,128)S(1)}, f32[16,1,128]{2,1,0:T(1,128)S(1)}, u32[]{:S(2)}, u32[]{:S(2)}) collective-permute-start(f32[16,1,128]{2,1,0:T(1,128)S(1)} %get-tuple-element.268), channel_id=1, source_target_pairs={{0,4},{4,8},{8,12},{12,16},{16,20},{20,24},{24,28},{1,5},{5,9},{9,... | collective-permute-start | bytes 24584 | tf_op jit(solution)/shard_map/ppermute | solution.py:23
  100.2 4.2 %collective-permute-done.13 = f32[16,1,128]{2,1,0:T(1,128)S(1)} collective-permute-done((f32[16,1,128]{2,1,0:T(1,128)S(1)}, f32[16,1,128]{2,1,0:T(1,128)S(1)}, u32[]{:S(2)}, u32[]{:S(2)}) %collective-permute-start.13) | collective-permute-done | bytes 8224 | tf_op jit(solution)/shard_map/ppermute | solution.py:25
  106.9 2.6 collective-permute-start.14
  112.3 2.6 reshape.46
  114.9 2.6 reduce_sum.29
  117.6 9.1 %all_gather.11 = f32[16,4,32]{0,1,2:T(4,128)S(1)} all-gather(f32[16,4,8]{0,1,2:T(4,128)S(1)} %copy.292), channel_id=1, replica_groups=mesh['row'=8,'col'=4] {'col'}, dimensions={2}, use_global_device_ids=true | all-gather | bytes 10240 | tf_op jit(solution)/shard_map/all_gather | solution.py:137
  129.0 2.1 select_maximum_fusion.12
  131.2 1.9 fusion.61
  133.0 3.7 %reshape.44 = f32[16,4,16,8,16]{4,3,2,1,0:T(8,128)} reshape(f32[16,64,128]{2,1,0:T(8,128)} %fusion.61) | data formatting | bytes 1048576 | tf_op jit(solution)/shard_map/reshape | solution.py:131
  136.7 2.6 reduce_sum.27
  139.4 5.5 %all_gather.9 = f32[16,4,32]{0,1,2:T(4,128)S(1)} all-gather(f32[16,4,8]{0,1,2:T(4,128)S(1)} %copy.279), channel_id=1, replica_groups=mesh['row'=8,'col'=4] {'col'}, dimensions={2}, use_global_device_ids=true | all-gather | bytes 10240 | tf_op jit(solution)/shard_map/all_gather | solution.py:135
  147.0 5.4 %collective-permute-start.21 = (f32[16,1,32]{2,1,0:T(1,128)S(1)}, f32[16,1,32]{2,1,0:T(1,128)S(1)}, u32[]{:S(2)}, u32[]{:S(2)}) collective-permute-start(f32[16,1,32]{2,1,0:T(1,128)S(1)} %get-tuple-element.290), channel_id=1, source_target_pairs={{0,4},{4,8},{8,12},{12,16},{16,20},{20,24},{24,28},{1,5},{5,9},{9,... | collective-permute-start | bytes 6152 | tf_op jit(solution)/shard_map/ppermute | solution.py:23
  155.7 5.4 %collective-permute-start.23 = (f32[16,1,32]{2,1,0:T(1,128)S(1)}, f32[16,1,32]{2,1,0:T(1,128)S(1)}, u32[]{:S(2)}, u32[]{:S(2)}) collective-permute-start(f32[16,1,32]{2,1,0:T(1,128)S(1)} %get-tuple-element.288), channel_id=1, source_target_pairs={{0,4},{4,8},{8,12},{12,16},{16,20},{20,24},{24,28},{1,5},{5,9},{9,... | collective-permute-start | bytes 6152 | tf_op jit(solution)/shard_map/ppermute | solution.py:23
  164.4 5.7 %collective-permute-start.25 = (f32[16,1,32]{2,1,0:T(1,128)S(1)}, f32[16,1,32]{2,1,0:T(1,128)S(1)}, u32[]{:S(2)}, u32[]{:S(2)}) collective-permute-start(f32[16,1,32]{2,1,0:T(1,128)S(1)} %get-tuple-element.286), channel_id=1, source_target_pairs={{0,4},{4,8},{8,12},{12,16},{16,20},{20,24},{24,28},{1,5},{5,9},{9,... | collective-permute-start | bytes 6152 | tf_op jit(solution)/shard_map/ppermute | solution.py:23
  173.3 5.7 %collective-permute-start.27 = (f32[16,1,32]{2,1,0:T(1,128)S(1)}, f32[16,1,32]{2,1,0:T(1,128)S(1)}, u32[]{:S(2)}, u32[]{:S(2)}) collective-permute-start(f32[16,1,32]{2,1,0:T(1,128)S(1)} %get-tuple-element.284), channel_id=1, source_target_pairs={{0,4},{4,8},{8,12},{12,16},{16,20},{20,24},{24,28},{1,5},{5,9},{9,... | collective-permute-start | bytes 6152 | tf_op jit(solution)/shard_map/ppermute | solution.py:23
  182.3 5.7 %collective-permute-start.29 = (f32[16,1,32]{2,1,0:T(1,128)S(1)}, f32[16,1,32]{2,1,0:T(1,128)S(1)}, u32[]{:S(2)}, u32[]{:S(2)}) collective-permute-start(f32[16,1,32]{2,1,0:T(1,128)S(1)} %get-tuple-element.282), channel_id=1, source_target_pairs={{0,4},{4,8},{8,12},{12,16},{16,20},{20,24},{24,28},{1,5},{5,9},{9,... | collective-permute-start | bytes 6152 | tf_op jit(solution)/shard_map/ppermute | solution.py:23
  191.3 5.7 %collective-permute-start.31 = (f32[16,1,32]{2,1,0:T(1,128)S(1)}, f32[16,1,32]{2,1,0:T(1,128)S(1)}, u32[]{:S(2)}, u32[]{:S(2)}) collective-permute-start(f32[16,1,32]{2,1,0:T(1,128)S(1)} %get-tuple-element.280), channel_id=1, source_target_pairs={{0,4},{4,8},{8,12},{12,16},{16,20},{20,24},{24,28},{1,5},{5,9},{9,... | collective-permute-start | bytes 6152 | tf_op jit(solution)/shard_map/ppermute | solution.py:23
  200.8 5.7 %collective-permute-start.33 = (f32[16,1,32]{2,1,0:T(1,128)S(1)}, f32[16,1,32]{2,1,0:T(1,128)S(1)}, u32[]{:S(2)}, u32[]{:S(2)}) collective-permute-start(f32[16,1,32]{2,1,0:T(1,128)S(1)} %get-tuple-element.278), channel_id=1, source_target_pairs={{0,4},{4,8},{8,12},{12,16},{16,20},{20,24},{24,28},{1,5},{5,9},{9,... | collective-permute-start | bytes 6152 | tf_op jit(solution)/shard_map/ppermute | solution.py:23
  208.5 2.4 broadcast_in_dim.76
  210.9 3.9 %reshape.47 = f32[16,64,128]{2,1,0:T(8,128)} reshape(f32[16,4,16,8,16]{4,3,2,1,0:T(8,128)} %broadcast_in_dim.76) | data formatting | bytes 1048576 | tf_op jit(solution)/shard_map/reshape | solution.py:147
  216.1 5.1 %collective-permute-start.34 = (f32[16,1,128]{2,1,0:T(1,128)S(1)}, f32[16,1,128]{2,1,0:T(1,128)S(1)}, u32[]{:S(2)}, u32[]{:S(2)}) collective-permute-start(f32[16,1,128]{2,1,0:T(1,128)S(1)} %get-tuple-element.266), channel_id=1, source_target_pairs={{0,4},{4,8},{8,12},{12,16},{16,20},{20,24},{24,28},{1,5},{5,9},{9,... | collective-permute-start | bytes 24584 | tf_op jit(solution)/shard_map/ppermute | solution.py:23
  222.6 5.4 %collective-permute-done.35 = f32[16,1,128]{2,1,0:T(1,128)S(1)} collective-permute-done((f32[16,1,128]{2,1,0:T(1,128)S(1)}, f32[16,1,128]{2,1,0:T(1,128)S(1)}, u32[]{:S(2)}, u32[]{:S(2)}) %collective-permute-start.35) | collective-permute-done | bytes 8224 | tf_op jit(solution)/shard_map/ppermute | solution.py:25
  235.7 2.4 collective-permute-done.37
  239.3 2.1 select_maximum_fusion.8
  242.7 4.8 %collective-permute-start.38 = (f32[16,1,128]{2,1,0:T(1,128)S(1)}, f32[16,1,128]{2,1,0:T(1,128)S(1)}, u32[]{:S(2)}, u32[]{:S(2)}) collective-permute-start(f32[16,1,128]{2,1,0:T(1,128)S(1)} %get-tuple-element.264), channel_id=1, source_target_pairs={{0,4},{4,8},{8,12},{12,16},{16,20},{20,24},{24,28},{1,5},{5,9},{9,... | collective-permute-start | bytes 24584 | tf_op jit(solution)/shard_map/ppermute | solution.py:23
  248.8 4.2 %collective-permute-done.39 = f32[16,1,128]{2,1,0:T(1,128)S(1)} collective-permute-done((f32[16,1,128]{2,1,0:T(1,128)S(1)}, f32[16,1,128]{2,1,0:T(1,128)S(1)}, u32[]{:S(2)}, u32[]{:S(2)}) %collective-permute-start.39) | collective-permute-done | bytes 8224 | tf_op jit(solution)/shard_map/ppermute | solution.py:25
  255.6 2.9 collective-permute-start.40
  262.2 1.6 collective-permute-done.41
  265.0 2.1 select_maximum_fusion.4
  268.4 3.9 %collective-permute-start.42 = (f32[16,1,128]{2,1,0:T(1,128)S(1)}, f32[16,1,128]{2,1,0:T(1,128)S(1)}, u32[]{:S(2)}, u32[]{:S(2)}) collective-permute-start(f32[16,1,128]{2,1,0:T(1,128)S(1)} %get-tuple-element.262), channel_id=1, source_target_pairs={{0,4},{4,8},{8,12},{12,16},{16,20},{20,24},{24,28},{1,5},{5,9},{9,... | collective-permute-start | bytes 24584 | tf_op jit(solution)/shard_map/ppermute | solution.py:23
  273.7 4.2 %collective-permute-done.43 = f32[16,1,128]{2,1,0:T(1,128)S(1)} collective-permute-done((f32[16,1,128]{2,1,0:T(1,128)S(1)}, f32[16,1,128]{2,1,0:T(1,128)S(1)}, u32[]{:S(2)}, u32[]{:S(2)}) %collective-permute-start.43) | collective-permute-done | bytes 8224 | tf_op jit(solution)/shard_map/ppermute | solution.py:25
  280.4 3.2 %collective-permute-start.44 = (f32[16,66,1]{1,0,2:T(8,128)S(1)}, f32[16,66,1]{1,0,2:T(8,128)S(1)}, u32[]{:S(2)}, u32[]{:S(2)}) collective-permute-start(f32[16,66,1]{1,0,2:T(8,128)S(1)} %copy.315), channel_id=1, source_target_pairs={{0,1},{1,2},{2,3},{4,5},{5,6},{6,7},{8,9},{9,10},{10,11},{12,13},{... | collective-permute-start | bytes 12680 | tf_op jit(solution)/shard_map/ppermute | solution.py:23
  289.8 2.1 select_maximum_fusion
  292.0 1.8 fusion.4
  (375 shorter events, 93.2 us)
Async XLA Ops:
  0.6 15.3 %copy-start.31 = (f32[16,64,128]{2,1,0:T(8,128)S(1)}, f32[16,64,128]{2,1,0:T(8,128)}, u32[]{:S(2)}) copy-start(f32[16,64,128]{2,1,0:T(8,128)} %param.8) | copy-start | bytes 1572868
  9.8 13.9 %collective-permute-start = (f32[16,1,128]{2,1,0:T(1,128)S(1)}, f32[16,1,128]{2,1,0:T(1,128)S(1)}, u32[]{:S(2)}, u32[]{:S(2)}) collective-permute-start(f32[16,1,128]{2,1,0:T(1,128)S(1)} %get-tuple-element.272), channel_id=1, source_target_pairs={{0,4},{4,8},{8,12},{12,16},{16,20},{20,24},{24,28},{1,5},{5,9},{9,... | collective-permute-start | bytes 24584 | tf_op jit(solution)/shard_map/ppermute | solution.py:23
  14.7 9.1 %collective-permute-start.1 = (f32[16,1,128]{2,1,0:T(1,128)S(1)}, f32[16,1,128]{2,1,0:T(1,128)S(1)}, u32[]{:S(2)}, u32[]{:S(2)}) collective-permute-start(f32[16,1,128]{2,1,0:T(1,128)S(1)} %get-tuple-element.273), channel_id=1, source_target_pairs={{4,0},{8,4},{12,8},{16,12},{20,16},{24,20},{28,24},{5,1},{9,5},{13... | collective-permute-start | bytes 24584 | tf_op jit(solution)/shard_map/ppermute | solution.py:25
  16.0 11.1 %collective-permute-start.4 = (f32[16,1,128]{2,1,0:T(1,128)S(1)}, f32[16,1,128]{2,1,0:T(1,128)S(1)}, u32[]{:S(2)}, u32[]{:S(2)}) collective-permute-start(f32[16,1,128]{2,1,0:T(1,128)S(1)} %get-tuple-element.274), channel_id=1, source_target_pairs={{0,4},{4,8},{8,12},{12,16},{16,20},{20,24},{24,28},{1,5},{5,9},{9,... | collective-permute-start | bytes 24584 | tf_op jit(solution)/shard_map/ppermute | solution.py:23
  20.5 6.6 %collective-permute-start.5 = (f32[16,1,128]{2,1,0:T(1,128)S(1)}, f32[16,1,128]{2,1,0:T(1,128)S(1)}, u32[]{:S(2)}, u32[]{:S(2)}) collective-permute-start(f32[16,1,128]{2,1,0:T(1,128)S(1)} %get-tuple-element.275), channel_id=1, source_target_pairs={{4,0},{8,4},{12,8},{16,12},{20,16},{24,20},{28,24},{5,1},{9,5},{13... | collective-permute-start | bytes 24584 | tf_op jit(solution)/shard_map/ppermute | solution.py:25
  22.4 76.4 %collective-permute-start.17 = (f32[16,1,32]{2,1,0:T(1,128)}, f32[16,1,32]{2,1,0:T(1,128)S(1)}, u32[]{:S(2)}, u32[]{:S(2)}) collective-permute-start(f32[16,1,32]{2,1,0:T(1,128)} %broadcast.79), channel_id=1, source_target_pairs={{4,0},{8,4},{12,8},{16,12},{20,16},{24,20},{28,24},{5,1},{9,5},{13... | collective-permute-start | bytes 6152 | tf_op jit(solution)/shard_map/ppermute | solution.py:25
  24.3 15.7 %collective-permute-start.2 = (f32[16,66,1]{1,0,2:T(8,128)S(1)}, f32[16,66,1]{1,0,2:T(8,128)S(1)}, u32[]{:S(2)}, u32[]{:S(2)}) collective-permute-start(f32[16,66,1]{1,0,2:T(8,128)S(1)} %copy.255), channel_id=1, source_target_pairs={{0,1},{1,2},{2,3},{4,5},{5,6},{6,7},{8,9},{9,10},{10,11},{12,13},{... | collective-permute-start | bytes 12680 | tf_op jit(solution)/shard_map/ppermute | solution.py:23
  25.8 20.1 %collective-permute-start.3 = (f32[16,66,1]{1,0,2:T(8,128)S(1)}, f32[16,66,1]{1,0,2:T(8,128)S(1)}, u32[]{:S(2)}, u32[]{:S(2)}) collective-permute-start(f32[16,66,1]{1,0,2:T(8,128)S(1)} %copy.256), channel_id=1, source_target_pairs={{1,0},{2,1},{3,2},{5,4},{6,5},{7,6},{9,8},{10,9},{11,10},{13,12},{... | collective-permute-start | bytes 12680 | tf_op jit(solution)/shard_map/ppermute | solution.py:25
  27.7 18.5 %collective-permute-start.6 = (f32[16,66,1]{1,0,2:T(8,128)S(1)}, f32[16,66,1]{1,0,2:T(8,128)S(1)}, u32[]{:S(2)}, u32[]{:S(2)}) collective-permute-start(f32[16,66,1]{1,0,2:T(8,128)S(1)} %copy.259), channel_id=1, source_target_pairs={{0,1},{1,2},{2,3},{4,5},{5,6},{6,7},{8,9},{9,10},{10,11},{12,13},{... | collective-permute-start | bytes 12680 | tf_op jit(solution)/shard_map/ppermute | solution.py:23
  32.7 13.8 %collective-permute-start.7 = (f32[16,66,1]{1,0,2:T(8,128)S(1)}, f32[16,66,1]{1,0,2:T(8,128)S(1)}, u32[]{:S(2)}, u32[]{:S(2)}) collective-permute-start(f32[16,66,1]{1,0,2:T(8,128)S(1)} %copy.260), channel_id=1, source_target_pairs={{1,0},{2,1},{3,2},{5,4},{6,5},{7,6},{9,8},{10,9},{11,10},{13,12},{... | collective-permute-start | bytes 12680 | tf_op jit(solution)/shard_map/ppermute | solution.py:25
  40.0 60.1 %collective-permute-start.19 = (f32[16,1,32]{2,1,0:T(1,128)}, f32[16,1,32]{2,1,0:T(1,128)S(1)}, u32[]{:S(2)}, u32[]{:S(2)}) collective-permute-start(f32[16,1,32]{2,1,0:T(1,128)} %broadcast.79), channel_id=1, source_target_pairs={{0,4},{4,8},{8,12},{12,16},{16,20},{20,24},{24,28},{1,5},{5,9},{9,... | collective-permute-start | bytes 6152 | tf_op jit(solution)/shard_map/ppermute | solution.py:23
  59.8 13.4 %collective-permute-start.8 = (f32[16,1,128]{2,1,0:T(1,128)S(1)}, f32[16,1,128]{2,1,0:T(1,128)S(1)}, u32[]{:S(2)}, u32[]{:S(2)}) collective-permute-start(f32[16,1,128]{2,1,0:T(1,128)S(1)} %get-tuple-element.270), channel_id=1, source_target_pairs={{0,4},{4,8},{8,12},{12,16},{16,20},{20,24},{24,28},{1,5},{5,9},{9,... | collective-permute-start | bytes 24584 | tf_op jit(solution)/shard_map/ppermute | solution.py:23
  64.6 8.6 %collective-permute-start.9 = (f32[16,1,128]{2,1,0:T(1,128)S(1)}, f32[16,1,128]{2,1,0:T(1,128)S(1)}, u32[]{:S(2)}, u32[]{:S(2)}) collective-permute-start(f32[16,1,128]{2,1,0:T(1,128)S(1)} %get-tuple-element.271), channel_id=1, source_target_pairs={{4,0},{8,4},{12,8},{16,12},{20,16},{24,20},{28,24},{5,1},{9,5},{13... | collective-permute-start | bytes 24584 | tf_op jit(solution)/shard_map/ppermute | solution.py:25
  76.8 6.3 %collective-permute-start.10 = (f32[16,66,1]{1,0,2:T(8,128)S(1)}, f32[16,66,1]{1,0,2:T(8,128)S(1)}, u32[]{:S(2)}, u32[]{:S(2)}) collective-permute-start(f32[16,66,1]{1,0,2:T(8,128)S(1)} %copy.267), channel_id=1, source_target_pairs={{0,1},{1,2},{2,3},{4,5},{5,6},{6,7},{8,9},{9,10},{10,11},{12,13},{... | collective-permute-start | bytes 12680 | tf_op jit(solution)/shard_map/ppermute | solution.py:23
  80.4 9.0 %collective-permute-start.11 = (f32[16,66,1]{1,0,2:T(8,128)S(1)}, f32[16,66,1]{1,0,2:T(8,128)S(1)}, u32[]{:S(2)}, u32[]{:S(2)}) collective-permute-start(f32[16,66,1]{1,0,2:T(8,128)S(1)} %copy.268), channel_id=1, source_target_pairs={{1,0},{2,1},{3,2},{5,4},{6,5},{7,6},{9,8},{10,9},{11,10},{13,12},{... | collective-permute-start | bytes 12680 | tf_op jit(solution)/shard_map/ppermute | solution.py:25
  81.7 30.4 %collective-permute-start.16 = (f32[16,1,32]{2,1,0:T(1,128)S(1)}, f32[16,1,32]{2,1,0:T(1,128)S(1)}, u32[]{:S(2)}, u32[]{:S(2)}) collective-permute-start(f32[16,1,32]{2,1,0:T(1,128)S(1)} %get-tuple-element.293), channel_id=1, source_target_pairs={{4,0},{8,4},{12,8},{16,12},{20,16},{24,20},{28,24},{5,1},{9,5},{13... | collective-permute-start | bytes 6152 | tf_op jit(solution)/shard_map/ppermute | solution.py:25
  83.1 29.1 %collective-permute-start.18 = (f32[16,1,32]{2,1,0:T(1,128)S(1)}, f32[16,1,32]{2,1,0:T(1,128)S(1)}, u32[]{:S(2)}, u32[]{:S(2)}) collective-permute-start(f32[16,1,32]{2,1,0:T(1,128)S(1)} %get-tuple-element.292), channel_id=1, source_target_pairs={{0,4},{4,8},{8,12},{12,16},{16,20},{20,24},{24,28},{1,5},{5,9},{9,... | collective-permute-start | bytes 6152 | tf_op jit(solution)/shard_map/ppermute | solution.py:23
  94.0 6.2 %collective-permute-start.12 = (f32[16,1,128]{2,1,0:T(1,128)S(1)}, f32[16,1,128]{2,1,0:T(1,128)S(1)}, u32[]{:S(2)}, u32[]{:S(2)}) collective-permute-start(f32[16,1,128]{2,1,0:T(1,128)S(1)} %get-tuple-element.268), channel_id=1, source_target_pairs={{0,4},{4,8},{8,12},{12,16},{16,20},{20,24},{24,28},{1,5},{5,9},{9,... | collective-permute-start | bytes 24584 | tf_op jit(solution)/shard_map/ppermute | solution.py:23
  98.8 5.5 %collective-permute-start.13 = (f32[16,1,128]{2,1,0:T(1,128)S(1)}, f32[16,1,128]{2,1,0:T(1,128)S(1)}, u32[]{:S(2)}, u32[]{:S(2)}) collective-permute-start(f32[16,1,128]{2,1,0:T(1,128)S(1)} %get-tuple-element.269), channel_id=1, source_target_pairs={{4,0},{8,4},{12,8},{16,12},{20,16},{24,20},{28,24},{5,1},{9,5},{13... | collective-permute-start | bytes 24584 | tf_op jit(solution)/shard_map/ppermute | solution.py:25
  106.9 19.8 %collective-permute-start.14 = (f32[16,66,1]{1,0,2:T(8,128)S(1)}, f32[16,66,1]{1,0,2:T(8,128)S(1)}, u32[]{:S(2)}, u32[]{:S(2)}) collective-permute-start(f32[16,66,1]{1,0,2:T(8,128)S(1)} %copy.273), channel_id=1, source_target_pairs={{0,1},{1,2},{2,3},{4,5},{5,6},{6,7},{8,9},{9,10},{10,11},{12,13},{... | collective-permute-start | bytes 12680 | tf_op jit(solution)/shard_map/ppermute | solution.py:23
  110.9 17.0 %collective-permute-start.15 = (f32[16,66,1]{1,0,2:T(8,128)S(1)}, f32[16,66,1]{1,0,2:T(8,128)S(1)}, u32[]{:S(2)}, u32[]{:S(2)}) collective-permute-start(f32[16,66,1]{1,0,2:T(8,128)S(1)} %copy.274), channel_id=1, source_target_pairs={{1,0},{2,1},{3,2},{5,4},{6,5},{7,6},{9,8},{10,9},{11,10},{13,12},{... | collective-permute-start | bytes 12680 | tf_op jit(solution)/shard_map/ppermute | solution.py:25
  145.7 6.8 %collective-permute-start.20 = (f32[16,1,32]{2,1,0:T(1,128)S(1)}, f32[16,1,32]{2,1,0:T(1,128)S(1)}, u32[]{:S(2)}, u32[]{:S(2)}) collective-permute-start(f32[16,1,32]{2,1,0:T(1,128)S(1)} %get-tuple-element.291), channel_id=1, source_target_pairs={{4,0},{8,4},{12,8},{16,12},{20,16},{24,20},{28,24},{5,1},{9,5},{13... | collective-permute-start | bytes 6152 | tf_op jit(solution)/shard_map/ppermute | solution.py:25
  147.0 6.8 %collective-permute-start.21 = (f32[16,1,32]{2,1,0:T(1,128)S(1)}, f32[16,1,32]{2,1,0:T(1,128)S(1)}, u32[]{:S(2)}, u32[]{:S(2)}) collective-permute-start(f32[16,1,32]{2,1,0:T(1,128)S(1)} %get-tuple-element.290), channel_id=1, source_target_pairs={{0,4},{4,8},{8,12},{12,16},{16,20},{20,24},{24,28},{1,5},{5,9},{9,... | collective-permute-start | bytes 6152 | tf_op jit(solution)/shard_map/ppermute | solution.py:23
  154.4 6.8 %collective-permute-start.22 = (f32[16,1,32]{2,1,0:T(1,128)S(1)}, f32[16,1,32]{2,1,0:T(1,128)S(1)}, u32[]{:S(2)}, u32[]{:S(2)}) collective-permute-start(f32[16,1,32]{2,1,0:T(1,128)S(1)} %get-tuple-element.289), channel_id=1, source_target_pairs={{4,0},{8,4},{12,8},{16,12},{20,16},{24,20},{28,24},{5,1},{9,5},{13... | collective-permute-start | bytes 6152 | tf_op jit(solution)/shard_map/ppermute | solution.py:25
  155.7 6.8 %collective-permute-start.23 = (f32[16,1,32]{2,1,0:T(1,128)S(1)}, f32[16,1,32]{2,1,0:T(1,128)S(1)}, u32[]{:S(2)}, u32[]{:S(2)}) collective-permute-start(f32[16,1,32]{2,1,0:T(1,128)S(1)} %get-tuple-element.288), channel_id=1, source_target_pairs={{0,4},{4,8},{8,12},{12,16},{16,20},{20,24},{24,28},{1,5},{5,9},{9,... | collective-permute-start | bytes 6152 | tf_op jit(solution)/shard_map/ppermute | solution.py:23
  163.1 7.0 %collective-permute-start.24 = (f32[16,1,32]{2,1,0:T(1,128)S(1)}, f32[16,1,32]{2,1,0:T(1,128)S(1)}, u32[]{:S(2)}, u32[]{:S(2)}) collective-permute-start(f32[16,1,32]{2,1,0:T(1,128)S(1)} %get-tuple-element.287), channel_id=1, source_target_pairs={{4,0},{8,4},{12,8},{16,12},{20,16},{24,20},{28,24},{5,1},{9,5},{13... | collective-permute-start | bytes 6152 | tf_op jit(solution)/shard_map/ppermute | solution.py:25
  164.4 7.1 %collective-permute-start.25 = (f32[16,1,32]{2,1,0:T(1,128)S(1)}, f32[16,1,32]{2,1,0:T(1,128)S(1)}, u32[]{:S(2)}, u32[]{:S(2)}) collective-permute-start(f32[16,1,32]{2,1,0:T(1,128)S(1)} %get-tuple-element.286), channel_id=1, source_target_pairs={{0,4},{4,8},{8,12},{12,16},{16,20},{20,24},{24,28},{1,5},{5,9},{9,... | collective-permute-start | bytes 6152 | tf_op jit(solution)/shard_map/ppermute | solution.py:23
  172.0 7.0 %collective-permute-start.26 = (f32[16,1,32]{2,1,0:T(1,128)S(1)}, f32[16,1,32]{2,1,0:T(1,128)S(1)}, u32[]{:S(2)}, u32[]{:S(2)}) collective-permute-start(f32[16,1,32]{2,1,0:T(1,128)S(1)} %get-tuple-element.285), channel_id=1, source_target_pairs={{4,0},{8,4},{12,8},{16,12},{20,16},{24,20},{28,24},{5,1},{9,5},{13... | collective-permute-start | bytes 6152 | tf_op jit(solution)/shard_map/ppermute | solution.py:25
  173.3 7.1 %collective-permute-start.27 = (f32[16,1,32]{2,1,0:T(1,128)S(1)}, f32[16,1,32]{2,1,0:T(1,128)S(1)}, u32[]{:S(2)}, u32[]{:S(2)}) collective-permute-start(f32[16,1,32]{2,1,0:T(1,128)S(1)} %get-tuple-element.284), channel_id=1, source_target_pairs={{0,4},{4,8},{8,12},{12,16},{16,20},{20,24},{24,28},{1,5},{5,9},{9,... | collective-permute-start | bytes 6152 | tf_op jit(solution)/shard_map/ppermute | solution.py:23
  181.0 7.0 %collective-permute-start.28 = (f32[16,1,32]{2,1,0:T(1,128)S(1)}, f32[16,1,32]{2,1,0:T(1,128)S(1)}, u32[]{:S(2)}, u32[]{:S(2)}) collective-permute-start(f32[16,1,32]{2,1,0:T(1,128)S(1)} %get-tuple-element.283), channel_id=1, source_target_pairs={{4,0},{8,4},{12,8},{16,12},{20,16},{24,20},{28,24},{5,1},{9,5},{13... | collective-permute-start | bytes 6152 | tf_op jit(solution)/shard_map/ppermute | solution.py:25
  182.3 7.1 %collective-permute-start.29 = (f32[16,1,32]{2,1,0:T(1,128)S(1)}, f32[16,1,32]{2,1,0:T(1,128)S(1)}, u32[]{:S(2)}, u32[]{:S(2)}) collective-permute-start(f32[16,1,32]{2,1,0:T(1,128)S(1)} %get-tuple-element.282), channel_id=1, source_target_pairs={{0,4},{4,8},{8,12},{12,16},{16,20},{20,24},{24,28},{1,5},{5,9},{9,... | collective-permute-start | bytes 6152 | tf_op jit(solution)/shard_map/ppermute | solution.py:23
  190.0 7.0 %collective-permute-start.30 = (f32[16,1,32]{2,1,0:T(1,128)S(1)}, f32[16,1,32]{2,1,0:T(1,128)S(1)}, u32[]{:S(2)}, u32[]{:S(2)}) collective-permute-start(f32[16,1,32]{2,1,0:T(1,128)S(1)} %get-tuple-element.281), channel_id=1, source_target_pairs={{4,0},{8,4},{12,8},{16,12},{20,16},{24,20},{28,24},{5,1},{9,5},{13... | collective-permute-start | bytes 6152 | tf_op jit(solution)/shard_map/ppermute | solution.py:25
  191.3 7.1 %collective-permute-start.31 = (f32[16,1,32]{2,1,0:T(1,128)S(1)}, f32[16,1,32]{2,1,0:T(1,128)S(1)}, u32[]{:S(2)}, u32[]{:S(2)}) collective-permute-start(f32[16,1,32]{2,1,0:T(1,128)S(1)} %get-tuple-element.280), channel_id=1, source_target_pairs={{0,4},{4,8},{8,12},{12,16},{16,20},{20,24},{24,28},{1,5},{5,9},{9,... | collective-permute-start | bytes 6152 | tf_op jit(solution)/shard_map/ppermute | solution.py:23
  199.5 7.0 %collective-permute-start.32 = (f32[16,1,32]{2,1,0:T(1,128)}, f32[16,1,32]{2,1,0:T(1,128)S(1)}, u32[]{:S(2)}, u32[]{:S(2)}) collective-permute-start(f32[16,1,32]{2,1,0:T(1,128)} %get-tuple-element.279), channel_id=1, source_target_pairs={{4,0},{8,4},{12,8},{16,12},{20,16},{24,20},{28,24},{5,1},{9,5},{13... | collective-permute-start | bytes 6152 | tf_op jit(solution)/shard_map/ppermute | solution.py:25
  200.8 7.1 %collective-permute-start.33 = (f32[16,1,32]{2,1,0:T(1,128)S(1)}, f32[16,1,32]{2,1,0:T(1,128)S(1)}, u32[]{:S(2)}, u32[]{:S(2)}) collective-permute-start(f32[16,1,32]{2,1,0:T(1,128)S(1)} %get-tuple-element.278), channel_id=1, source_target_pairs={{0,4},{4,8},{8,12},{12,16},{16,20},{20,24},{24,28},{1,5},{5,9},{9,... | collective-permute-start | bytes 6152 | tf_op jit(solution)/shard_map/ppermute | solution.py:23
  216.1 11.9 %copy-start.10 = (f32[16,64,128]{2,1,0:T(8,128)}, f32[16,64,128]{2,1,0:T(8,128)S(1)}, u32[]{:S(2)}) copy-start(f32[16,64,128]{2,1,0:T(8,128)S(1)} %add.4249) | copy-start | bytes 1572868
  216.1 6.4 %collective-permute-start.34 = (f32[16,1,128]{2,1,0:T(1,128)S(1)}, f32[16,1,128]{2,1,0:T(1,128)S(1)}, u32[]{:S(2)}, u32[]{:S(2)}) collective-permute-start(f32[16,1,128]{2,1,0:T(1,128)S(1)} %get-tuple-element.266), channel_id=1, source_target_pairs={{0,4},{4,8},{8,12},{12,16},{16,20},{20,24},{24,28},{1,5},{5,9},{9,... | collective-permute-start | bytes 24584 | tf_op jit(solution)/shard_map/ppermute | solution.py:23
  221.2 6.7 %collective-permute-start.35 = (f32[16,1,128]{2,1,0:T(1,128)S(1)}, f32[16,1,128]{2,1,0:T(1,128)S(1)}, u32[]{:S(2)}, u32[]{:S(2)}) collective-permute-start(f32[16,1,128]{2,1,0:T(1,128)S(1)} %get-tuple-element.267), channel_id=1, source_target_pairs={{4,0},{8,4},{12,8},{16,12},{20,16},{24,20},{28,24},{5,1},{9,5},{13... | collective-permute-start | bytes 24584 | tf_op jit(solution)/shard_map/ppermute | solution.py:25
  230.5 4.1 %collective-permute-start.36 = (f32[16,66,1]{1,0,2:T(8,128)S(1)}, f32[16,66,1]{1,0,2:T(8,128)S(1)}, u32[]{:S(2)}, u32[]{:S(2)}) collective-permute-start(f32[16,66,1]{1,0,2:T(8,128)S(1)} %copy.303), channel_id=1, source_target_pairs={{0,1},{1,2},{2,3},{4,5},{5,6},{6,7},{8,9},{9,10},{10,11},{12,13},{... | collective-permute-start | bytes 12680 | tf_op jit(solution)/shard_map/ppermute | solution.py:23
  233.1 5.0 %collective-permute-start.37 = (f32[16,66,1]{1,0,2:T(8,128)S(1)}, f32[16,66,1]{1,0,2:T(8,128)S(1)}, u32[]{:S(2)}, u32[]{:S(2)}) collective-permute-start(f32[16,66,1]{1,0,2:T(8,128)S(1)} %copy.304), channel_id=1, source_target_pairs={{1,0},{2,1},{3,2},{5,4},{6,5},{7,6},{9,8},{10,9},{11,10},{13,12},{... | collective-permute-start | bytes 12680 | tf_op jit(solution)/shard_map/ppermute | solution.py:25
  242.7 6.2 %collective-permute-start.38 = (f32[16,1,128]{2,1,0:T(1,128)S(1)}, f32[16,1,128]{2,1,0:T(1,128)S(1)}, u32[]{:S(2)}, u32[]{:S(2)}) collective-permute-start(f32[16,1,128]{2,1,0:T(1,128)S(1)} %get-tuple-element.264), channel_id=1, source_target_pairs={{0,4},{4,8},{8,12},{12,16},{16,20},{20,24},{24,28},{1,5},{5,9},{9,... | collective-permute-start | bytes 24584 | tf_op jit(solution)/shard_map/ppermute | solution.py:23
  247.5 5.5 %collective-permute-start.39 = (f32[16,1,128]{2,1,0:T(1,128)S(1)}, f32[16,1,128]{2,1,0:T(1,128)S(1)}, u32[]{:S(2)}, u32[]{:S(2)}) collective-permute-start(f32[16,1,128]{2,1,0:T(1,128)S(1)} %get-tuple-element.265), channel_id=1, source_target_pairs={{4,0},{8,4},{12,8},{16,12},{20,16},{24,20},{28,24},{5,1},{9,5},{13... | collective-permute-start | bytes 24584 | tf_op jit(solution)/shard_map/ppermute | solution.py:25
  255.6 5.5 %collective-permute-start.40 = (f32[16,66,1]{1,0,2:T(8,128)S(1)}, f32[16,66,1]{1,0,2:T(8,128)S(1)}, u32[]{:S(2)}, u32[]{:S(2)}) collective-permute-start(f32[16,66,1]{1,0,2:T(8,128)S(1)} %copy.309), channel_id=1, source_target_pairs={{0,1},{1,2},{2,3},{4,5},{5,6},{6,7},{8,9},{9,10},{10,11},{12,13},{... | collective-permute-start | bytes 12680 | tf_op jit(solution)/shard_map/ppermute | solution.py:23
  259.8 4.1 %collective-permute-start.41 = (f32[16,66,1]{1,0,2:T(8,128)S(1)}, f32[16,66,1]{1,0,2:T(8,128)S(1)}, u32[]{:S(2)}, u32[]{:S(2)}) collective-permute-start(f32[16,66,1]{1,0,2:T(8,128)S(1)} %copy.310), channel_id=1, source_target_pairs={{1,0},{2,1},{3,2},{5,4},{6,5},{7,6},{9,8},{10,9},{11,10},{13,12},{... | collective-permute-start | bytes 12680 | tf_op jit(solution)/shard_map/ppermute | solution.py:25
  268.4 5.3 %collective-permute-start.42 = (f32[16,1,128]{2,1,0:T(1,128)S(1)}, f32[16,1,128]{2,1,0:T(1,128)S(1)}, u32[]{:S(2)}, u32[]{:S(2)}) collective-permute-start(f32[16,1,128]{2,1,0:T(1,128)S(1)} %get-tuple-element.262), channel_id=1, source_target_pairs={{0,4},{4,8},{8,12},{12,16},{16,20},{20,24},{24,28},{1,5},{5,9},{9,... | collective-permute-start | bytes 24584 | tf_op jit(solution)/shard_map/ppermute | solution.py:23
  272.3 5.5 %collective-permute-start.43 = (f32[16,1,128]{2,1,0:T(1,128)S(1)}, f32[16,1,128]{2,1,0:T(1,128)S(1)}, u32[]{:S(2)}, u32[]{:S(2)}) collective-permute-start(f32[16,1,128]{2,1,0:T(1,128)S(1)} %get-tuple-element.263), channel_id=1, source_target_pairs={{4,0},{8,4},{12,8},{16,12},{20,16},{24,20},{28,24},{5,1},{9,5},{13... | collective-permute-start | bytes 24584 | tf_op jit(solution)/shard_map/ppermute | solution.py:25
  280.4 5.8 %collective-permute-start.44 = (f32[16,66,1]{1,0,2:T(8,128)S(1)}, f32[16,66,1]{1,0,2:T(8,128)S(1)}, u32[]{:S(2)}, u32[]{:S(2)}) collective-permute-start(f32[16,66,1]{1,0,2:T(8,128)S(1)} %copy.315), channel_id=1, source_target_pairs={{0,1},{1,2},{2,3},{4,5},{5,6},{6,7},{8,9},{9,10},{10,11},{12,13},{... | collective-permute-start | bytes 12680 | tf_op jit(solution)/shard_map/ppermute | solution.py:23
  284.9 3.8 %collective-permute-start.45 = (f32[16,66,1]{1,0,2:T(8,128)S(1)}, f32[16,66,1]{1,0,2:T(8,128)S(1)}, u32[]{:S(2)}, u32[]{:S(2)}) collective-permute-start(f32[16,66,1]{1,0,2:T(8,128)S(1)} %copy.316), channel_id=1, source_target_pairs={{1,0},{2,1},{3,2},{5,4},{6,5},{7,6},{9,8},{10,9},{11,10},{13,12},{... | collective-permute-start | bytes 12680 | tf_op jit(solution)/shard_map/ppermute | solution.py:25
  (38 other events, 100.7 us)
where the time goes:
time: 300 us; the launch traced here: 294 us
  starting transfers between devices  131 us (44%)
  local copies, waits for them, and re-layouts  55.2 us (18%)
  other arithmetic  50.2 us (17%)
  waiting for transfers between devices  32.8 us (11%)
  blocking collectives  21.8 us (7%)
    ppermute x23, starting transfers between devices, padded_2(): lax.ppermute(tail, axis, [(i, (i + 1) % count) for i in range(ends)])  101 us
    ppermute x23, starting transfers between devices, padded_2(): lax.ppermute(head, axis, [((i + 1) % count, i) for i in range(ends)])  30 us
    ppermute x23, waiting for transfers between devices, padded_2(): lax.ppermute(head, axis, [((i + 1) % count, i) for i in range(ends)])  23.3 us
    concatenate x23, other arithmetic, padded_2(): jnp.concatenate([lax.ppermute(tail, axis, [(i, (i + 1) % count) for i in...  14.4 us
    slice x13, local copies, waits for them, and re-layouts, padded_2(): head = lax.slice_in_dim(cells, 0, width, axis=dim)  13.2 us
    add x4, other arithmetic, smooth(): field = field + OMEGA * (right_side - fine_apply(field, coefs, cap)) / diag  12.9 us
    ppermute x23, waiting for transfers between devices, padded_2(): lax.ppermute(tail, axis, [(i, (i + 1) % count) for i in range(ends)])  9.55 us
    all_gather x1, blocking collectives, shards(): lax.all_gather(capc, 'col', axis=2, tiled=True)  9.08 us
  transfers between devices with their start and end apart: 46, of which 14 were waited for; matrix products, arithmetic and copies ran while one was open for 16% of the time, Pallas kernels for 0%

commit v1 on v0

v1 whole, which is shorter than its diff:
```python
import functools
import math

import jax
import jax.numpy as jnp
from jax import lax
from jax.experimental import pallas as pl
from jax.experimental.pallas import tpu as pltpu
from jax.sharding import PartitionSpec as P

COARSEN = 16
PRE = 2
POST = 2
CSWEEPS = 8
OMEGA = 0.8
HALO = 8
LANES = 128
HIGH = lax.Precision.HIGHEST
MESH = pl.DeviceIdType.MESH


def lane_ids(shape):
    return lax.broadcasted_iota(jnp.int32, shape, len(shape) - 1)


def row_ids(shape):
    return lax.broadcasted_iota(jnp.int32, shape, len(shape) - 2)


def kernel(
    sizes,
    cond_ref, capa_ref, rhs_ref, guess_ref, mat_ref,
    out_ref, res_ref,
    va, vb, kap, cap, cz, cx, cy, rx, wgt, dia,
    mhalo, pack_l, pack_r, recv_l, recv_r, kl, kr,
    xsum, tile_k, tile_r, grid_k, grid_r,
    hx, hy, hup, hinv, hgain, hback, hres, ecor,
    fsend, frecv, ksend, krecv, rsend, rrecv,
):
    nrow, ncol, reach_r, reach_c = sizes
    depth, wx, wy = rhs_ref.shape
    ext = wx + 2 * HALO
    cells_x = wx // COARSEN
    cells_y = wy // COARSEN
    nclass = cond_ref.shape[0]
    row = lax.axis_index("row")
    col = lax.axis_index("col")
    rows_c = grid_r.shape[1]

    def exists(dr, dc):
        ok = (row + dr >= 0) & (row + dr < nrow)
        return ok & (col + dc >= 0) & (col + dc < ncol)

    def device(dr, dc):
        return (lax.rem(row + dr + nrow, nrow), lax.rem(col + dc + ncol, ncol))

    peers = [
        (dr, dc)
        for dr in range(-reach_r, reach_r + 1)
        for dc in range(-reach_c, reach_c + 1)
        if (dr, dc) != (0, 0)
    ]

    grid_k[...] = jnp.zeros_like(grid_k)
    grid_r[...] = jnp.zeros_like(grid_r)
    mhalo[...] = jnp.zeros_like(mhalo)
    recv_l[...] = jnp.zeros_like(recv_l)
    recv_r[...] = jnp.zeros_like(recv_r)
    lo, hi = slice(0, HALO), slice(ext - HALO, ext)
    own = slice(HALO, HALO + wx)
    for side in (lo, hi):
        va[1 : depth + 1, side, :wy] = jnp.zeros((depth, HALO, wy), jnp.float32)
        rx[:, side, :wy] = jnp.zeros((depth, HALO, wy), jnp.float32)

    barrier = pltpu.get_barrier_semaphore()
    for dr, dc in peers:
        @pl.when(exists(dr, dc))
        def _():
            pl.semaphore_signal(barrier, inc=1, device_id=device(dr, dc), device_id_type=MESH)

    lane = lane_ids((wx, LANES))
    for index, source in enumerate((guess_ref, rhs_ref, mat_ref)):
        left = jnp.zeros((wx, LANES), jnp.float32)
        right = jnp.zeros((wx, LANES), jnp.float32)
        for z in range(depth):
            plane = source[z].astype(jnp.float32)
            here = lane // 8 == z
            left = jnp.where(here, pltpu.roll(plane, (8 * z) % LANES, 1), left)
            right = jnp.where(here, pltpu.roll(plane, (8 * z + 8) % LANES, 1), right)
        pack_l[index] = left
        pack_r[index] = right

    tall_p = jnp.minimum(row + reach_r, nrow - 1) - jnp.maximum(row - reach_r, 0) + 1
    wide_p = jnp.minimum(col + reach_c, ncol - 1) - jnp.maximum(col - reach_c, 0) + 1
    pl.semaphore_wait(barrier, tall_p * wide_p - 1)

    zs = slice(1, depth + 1)
    last = slice(wx - HALO, wx)
    first = slice(0, HALO)
    plan = []
    for dr, src, dst in ((1, last, lo), (-1, first, hi)):
        plan.append((dr, 0, guess_ref.at[:, src, :], va.at[zs, dst, 0:wy]))
        plan.append((dr, 0, rhs_ref.at[:, src, :], rx.at[:, dst, 0:wy]))
        plan.append((dr, 0, mat_ref.at[:, src, :], mhalo.at[0 if dr == 1 else 1]))
    for dc, pack, recv in ((1, pack_r, recv_l), (-1, pack_l, recv_r)):
        plan.append((0, dc, pack, recv.at[:, own, :]))
        plan.append((1, dc, pack.at[:, last, :], recv.at[:, lo, :]))
        plan.append((-1, dc, pack.at[:, first, :], recv.at[:, hi, :]))
    fine = []
    for index, (dr, dc, src, dst) in enumerate(plan):
        copy = pltpu.make_async_remote_copy(
            src_ref=src, dst_ref=dst, send_sem=fsend.at[index], recv_sem=frecv.at[index],
            device_id=device(dr, dc), device_id_type=MESH,
        )
        fine.append((dr, dc, copy))

    def start_all(copies):
        for dr, dc, copy in copies:
            @pl.when(exists(dr, dc))
            def _():
                copy.start()

    def recv_all(copies):
        for dr, dc, copy in copies:
            @pl.when(exists(-dr, -dc))
            def _():
                copy.wait_recv()

    def sent_all(copies):
        for dr, dc, copy in copies:
            @pl.when(exists(dr, dc))
            def _():
                copy.wait_send()

    start_all(fine)

    def lookup(classes):
        kval = jnp.full(classes.shape, cond_ref[0], jnp.float32)
        cval = jnp.full(classes.shape, capa_ref[0], jnp.float32)
        for k in range(1, nclass):
            hit = classes == k
            kval = jnp.where(hit, cond_ref[k], kval)
            cval = jnp.where(hit, capa_ref[k], cval)
        return kval, cval

    def xblocks(plane):
        part = plane.reshape(cells_x, COARSEN // 8, 8, wy).sum(axis=1)
        return part.sum(axis=1)

    xsum[...] = jnp.zeros_like(xsum)

    def own_fields(z, carry):
        kval, cval = lookup(mat_ref[z])
        kap[z + 1, own, 0:wy] = kval
        cap[z, own, 0:wy] = cval
        rx[z, own, 0:wy] = rhs_ref[z]
        va[z + 1, own, 0:wy] = guess_ref[z]
        xsum[0, z, 0:cells_x, :] = xblocks(kval)
        xsum[1, z, 0:cells_x, :] = xblocks(cval)
        return carry

    lax.fori_loop(0, depth, own_fields, 0)

    gather_rows = lax.broadcasted_iota(jnp.int32, (wy, LANES), 0) // COARSEN
    summing = (gather_rows == lane_ids((wy, LANES)) % cells_y).astype(jnp.float32)
    zshape = (depth, 8, LANES)
    zmask = lane_ids(zshape) // cells_y == lax.broadcasted_iota(jnp.int32, zshape, 0)

    def coarse_tile(which):
        block = jnp.dot(xsum[which].reshape(depth * 8, wy), summing, precision=HIGH,
                        preferred_element_type=jnp.float32)
        return jnp.where(zmask, block.reshape(zshape), 0.0).sum(axis=0)[0:cells_x]

    def spread(tile, grid, sends, recvs):
        copies = []
        for index, (dr, dc) in enumerate(peers):
            at = cells_x * (reach_r - dr)
            copy = pltpu.make_async_remote_copy(
                src_ref=tile, dst_ref=grid.at[:, reach_c - dc, at : at + cells_x, :],
                send_sem=sends.at[index], recv_sem=recvs.at[index],
                device_id=device(dr, dc), device_id_type=MESH,
            )
            copies.append((dr, dc, copy))
        return copies

    mid = slice(cells_x * reach_r, cells_x * (reach_r + 1))
    gk = grid_k
    tile_k[0] = coarse_tile(0) * (1.0 / (COARSEN * COARSEN))
    tile_k[1] = coarse_tile(1)
    spread_k = spread(tile_k, gk, ksend, krecv)
    start_all(spread_k)
    gk[0, reach_c, mid, :] = tile_k[0]
    gk[1, reach_c, mid, :] = tile_k[1]

    recv_all(fine)
    for field, side_ok in ((0, exists(-1, 0)), (1, exists(1, 0))):
        at = lo if field == 0 else hi
        kval, cval = lookup(mhalo[field])
        kap[zs, at, 0:wy] = jnp.where(side_ok, kval, 0.0)
        cap[:, at, 0:wy] = jnp.where(side_ok, cval, 0.0)
    prow = row_ids((ext, LANES))
    rows_ok = ((prow >= HALO) | (row > 0)) & ((prow < ext - HALO) | (row < nrow - 1))
    for recv, keep, side_ok in ((recv_l, kl, col > 0), (recv_r, kr, col < ncol - 1)):
        kval, cval = lookup(recv[2].astype(jnp.int32))
        ok = rows_ok & side_ok
        keep[0] = jnp.where(ok, kval, 0.0)
        keep[1] = jnp.where(ok, cval, 0.0)
    elane = lane_ids((ext, LANES))
    rim = slice(wy, wy + LANES)
    for left, right, dst, first_z in (
        (kl.at[0], kr.at[0], kap, 1),
        (kl.at[1], kr.at[1], cap, 0),
        (recv_l.at[0], recv_r.at[0], va, 1),
        (recv_l.at[1], recv_r.at[1], rx, 0),
    ):
        lvals, rvals = left[...], right[...]
        for z in range(depth):
            shift = (LANES - 8 * z) % LANES
            a = pltpu.roll(rvals, shift, 1) if shift else rvals
            shift = (LANES - 8 - 8 * z) % LANES
            b = pltpu.roll(lvals, shift, 1) if shift else lvals
            dst[z + first_z, :, rim] = jnp.where(elane < 8, a, jnp.where(elane >= LANES - 8, b, 0.0))
    zero = jnp.zeros((ext, wy + LANES), jnp.float32)
    for field in (va, vb, kap):
        field[0] = zero
        field[depth + 1] = zero

    wide = wy + LANES

    def xnext(p):
        return pltpu.roll(p, ext - 1, 0)

    def xprev(p):
        return pltpu.roll(p, 1, 0)

    def ynext(p):
        return pltpu.roll(p, wide - 1, 1)

    def yprev(p):
        return pltpu.roll(p, 1, 1)

    cz[0] = 0.5 * kap[1]

    def coefs(z, carry):
        k = kap[z + 1]
        zc = 0.5 * (k + kap[z + 2])
        xc = 0.5 * (k + xnext(k))
        yc = 0.5 * (k + ynext(k))
        cz[z + 1] = zc
        cx[z] = xc
        cy[z] = yc
        d = cap[z] + zc
        d = d + cz[z]
        d = d + xc
        d = d + xprev(xc)
        d = d + yc
        d = d + yprev(yc)
        dia[z] = d
        wgt[z] = jnp.where(k > 0.0, OMEGA / d, 0.0)
        return carry

    lax.fori_loop(0, depth, coefs, 0)

    def around(src, z, v):
        t = rx[z] + cz[z + 1] * src[z + 2]
        t = t + cz[z] * src[z]
        xc = cx[z]
        t = t + xc * xnext(v)
        t = t + xprev(xc * v)
        yc = cy[z]
        t = t + yc * ynext(v)
        return t + yprev(yc * v)

    def clean(z, carry):
        va[z + 1] = jnp.where(kap[z + 1] > 0.0, va[z + 1], 0.0)
        return carry

    lax.fori_loop(0, depth, clean, 0)

    def sweep(src, dst):
        def body(z, carry):
            v = src[z + 1]
            dst[z + 1] = (1.0 - OMEGA) * v + wgt[z] * around(src, z, v)
            return carry

        lax.fori_loop(0, depth, body, 0)

    def inner_residual(src, z):
        v = src[z + 1]
        return (around(src, z, v) - dia[z] * v)[own, 0:wy]

    bufs = [va, vb]
    for _ in range(PRE):
        sweep(bufs[0], bufs[1])
        bufs.reverse()

    def restrict(z, carry):
        xsum[0, z, 0:cells_x, :] = xblocks(inner_residual(bufs[0], z))
        return carry

    lax.fori_loop(0, depth, restrict, 0)
    tile_r[0] = coarse_tile(0)
    spread_r = spread(tile_r, grid_r, rsend, rrecv)
    start_all(spread_r)
    grid_r[0, reach_c, mid, :] = tile_r[0]

    recv_all(spread_k)
    rows_w = grid_r.shape[2]
    wlane = lane_ids((rows_w, LANES))
    wrow = row_ids((rows_w, LANES))
    ncells_c = 2 * reach_c + 1
    crow = wrow + (row - reach_r) * cells_x
    ccol = wlane + (col - reach_c) * cells_y
    inside = (crow >= 0) & (crow < nrow * cells_x) & (ccol >= 0) & (ccol < ncol * cells_y)
    inside = inside & (wrow < (2 * reach_r + 1) * cells_x) & (wlane < ncells_c * cells_y)

    def window(grid, which, z):
        acc = jnp.zeros((rows_w, LANES), jnp.float32)
        for block in range(ncells_c):
            shift = (cells_y * (block - z)) % LANES
            part = grid[which, block]
            part = pltpu.roll(part, shift, 1) if shift else part
            acc = jnp.where(wlane // cells_y == block, part, acc)
        return jnp.where(inside, acc, 0.0)

    kb = [window(gk, 0, z) for z in range(depth)]
    factor = 0.5 * COARSEN * COARSEN
    below = factor * kb[0]
    gain = None
    for z in range(depth):
        k = kb[z]
        above = factor * (k + kb[z + 1]) if z + 1 < depth else factor * k
        xc = 0.5 * (k + pltpu.roll(k, rows_w - 1, 0))
        yc = 0.5 * (k + pltpu.roll(k, LANES - 1, 1))
        xm = pltpu.roll(xc, 1, 0)
        ym = pltpu.roll(yc, 1, 1)
        d = window(gk, 1, z) + above
        d = d + below
        d = d + xc
        d = d + xm
        d = d + yc
        d = d + ym
        upper = above if z + 1 < depth else jnp.zeros_like(above)
        denom = d if z == 0 else d - below * gain
        inv = jnp.where(inside, 1.0 / denom, 0.0)
        gain = upper * inv
        hx[z] = xc
        hy[z] = yc
        hinv[z] = inv
        hgain[z] = gain
        hback[z] = below * inv if z else jnp.zeros_like(inv)
        below = above

    recv_all(spread_r)
    for z in range(depth):
        hres[z] = window(grid_r, 0, z)
        ecor[z] = jnp.zeros((rows_w, LANES), jnp.float32)

    def coarse_sweep(step, carry):
        head = None
        heads = []
        for z in range(depth):
            e = ecor[z]
            xc, yc = hx[z], hy[z]
            r = hres[z] + xc * pltpu.roll(e, rows_w - 1, 0)
            r = r + pltpu.roll(xc * e, 1, 0)
            r = r + yc * pltpu.roll(e, LANES - 1, 1)
            r = r + pltpu.roll(yc * e, 1, 1)
            r = r * hinv[z]
            head = r if z == 0 else r + hback[z] * head
            heads.append(head)
        value = heads[-1]
        ecor[depth - 1] = value
        for z in range(depth - 2, -1, -1):
            value = heads[z] + hgain[z] * value
            ecor[z] = value
        return carry

    lax.fori_loop(0, CSWEEPS, coarse_sweep, 0)

    own_r = cells_x * reach_r
    low_r = (own_r - 1) // 8 * 8
    top_r = -(-(own_r + cells_x + 1) // 8) * 8
    ylane = lane_ids((LANES, wide))
    place = jnp.where(ylane < wy + LANES // 2, ylane // COARSEN, -1) + cells_y * reach_c
    picking = (lax.broadcasted_iota(jnp.int32, (LANES, wide), 0) == place).astype(jnp.float32)

    def prolong(z, carry):
        e = ecor[z, low_r:top_r, :]
        spread_y = jnp.dot(e, picking, precision=HIGH, preferred_element_type=jnp.float32)
        parts = []
        for cell in range(-1, cells_x + 1):
            at = own_r + cell - low_r
            tall = COARSEN if 0 <= cell < cells_x else HALO
            parts.append(jnp.broadcast_to(spread_y[at : at + 1, :], (tall, wide)))
        whole = jnp.concatenate(parts, axis=0)
        bufs[0][z + 1] = jnp.where(kap[z + 1] > 0.0, bufs[0][z + 1] + whole, 0.0)
        return carry

    lax.fori_loop(0, depth, prolong, 0)
    for _ in range(POST):
        sweep(bufs[0], bufs[1])
        bufs.reverse()

    def finish(z, carry):
        out_ref[z] = bufs[0][z + 1, own, 0:wy]
        res_ref[z] = inner_residual(bufs[0], z)
        return carry

    lax.fori_loop(0, depth, finish, 0)
    sent_all(fine)
    sent_all(spread_k)
    sent_all(spread_r)


def shards(nrow, ncol, right_side, guess, material, conductivity, capacity):
    depth, wx, wy = right_side.shape
    ext, wide = wx + 2 * HALO, wy + LANES
    cells_x, cells_y = wx // COARSEN, wy // COARSEN
    reach_r = min(math.ceil((CSWEEPS + 1) / cells_x), nrow - 1)
    reach_c = min(math.ceil((CSWEEPS + 1) / cells_y), ncol - 1)
    npeers = (2 * reach_r + 1) * (2 * reach_c + 1) - 1
    rows_w = -(-(2 * reach_r + 1) * cells_x // 8) * 8
    f32 = jnp.float32
    full = lambda planes: pltpu.VMEM((planes, ext, wide), f32)
    coarse = pltpu.VMEM((depth, rows_w, LANES), f32)
    dma = pltpu.SemaphoreType.DMA
    vmem = pl.BlockSpec(memory_space=pltpu.VMEM)
    smem = pl.BlockSpec(memory_space=pltpu.SMEM)
    shape = jax.ShapeDtypeStruct(right_side.shape, f32)
    return pl.pallas_call(
        functools.partial(kernel, (nrow, ncol, reach_r, reach_c)),
        out_shape=(shape, shape),
        in_specs=[smem, smem, vmem, vmem, vmem],
        out_specs=(vmem, vmem),
        scratch_shapes=[
            full(depth + 2), full(depth + 2), full(depth + 2), full(depth), full(depth + 1),
            full(depth), full(depth), full(depth), full(depth), full(depth),
            pltpu.VMEM((2, depth, HALO, wy), jnp.int32),
            pltpu.VMEM((3, wx, LANES), f32), pltpu.VMEM((3, wx, LANES), f32),
            pltpu.VMEM((3, ext, LANES), f32), pltpu.VMEM((3, ext, LANES), f32),
            pltpu.VMEM((2, ext, LANES), f32), pltpu.VMEM((2, ext, LANES), f32),
            pltpu.VMEM((2, depth, 8, wy), f32),
            pltpu.VMEM((2, cells_x, LANES), f32), pltpu.VMEM((1, cells_x, LANES), f32),
            pltpu.VMEM((2, 2 * reach_c + 1, rows_w, LANES), f32),
            pltpu.VMEM((1, 2 * reach_c + 1, rows_w, LANES), f32),
            coarse, coarse, coarse, coarse, coarse, coarse, coarse, coarse,
            dma((12,)), dma((12,)),
            dma((npeers,)), dma((npeers,)), dma((npeers,)), dma((npeers,)),
        ],
        compiler_params=pltpu.CompilerParams(
            collective_id=0, has_side_effects=True, vmem_limit_bytes=48 * 1024 * 1024
        ),
    )(conductivity, capacity, right_side, guess, material)


def solution(mesh):
    placed = (P(None, "row", "col"), P(None, "row", "col"), P(None, "row", "col"), P(), P())
    return jax.shard_map(
        functools.partial(shards, mesh.shape["row"], mesh.shape["col"]),
        mesh=mesh,
        in_specs=placed,
        out_specs=(P(None, "row", "col"), P(None, "row", "col")),
        check_vma=False,
    )
```

time: 300 us -> 51.4 us (0.17); the launches traced: 294 us -> 51.1 us
  starting transfers between devices: 131 us -> 0 us
  other arithmetic: 50.2 us -> 0 us
  local copies, waits for them, and re-layouts: 55.2 us -> 6.01 us
  Pallas kernels: 0 us -> 44.4 us
  waiting for transfers between devices: 32.8 us -> 0 us
  blocking collectives: 21.8 us -> 0 us
    ppermute x46 -> x0, starting transfers between devices: 131 us -> none  [the longest x23 101 us: padded_2(): lax.ppermute(tail, axis, [(i, (i + 1) % count) for i in range(ends)])]
    pallas_call x0 -> x1, Pallas kernels: none -> 44.4 us  [shards(): pl.pallas_call(functools.partial(kernel, (nrow, ncol, reach_r, reach_c)),...]
    ppermute x46 -> x0, waiting for transfers between devices: 32.8 us -> none  [the longest x23 23.3 us: padded_2(): lax.ppermute(head, axis, [((i + 1) % count, i) for i in range(ends)])]
    slice x38 -> x0, local copies, waits for them, and re-layouts: 23.5 us -> none  [the longest x13 13.2 us: padded_2(): head = lax.slice_in_dim(cells, 0, width, axis=dim)]
    all_gather x3 -> x0, blocking collectives: 21.8 us -> none  [the longest x1 9.08 us: shards(): lax.all_gather(capc, 'col', axis=2, tiled=True)]
    add x14 -> x0, other arithmetic: 15.2 us -> none  [the longest x4 12.9 us: smooth(): field = field + OMEGA * (right_side - fine_apply(field, coefs, cap)) / diag]
    concatenate x23 -> x0, other arithmetic: 14.4 us -> none  [padded_2(): jnp.concatenate([lax.ppermute(tail, axis, [(i, (i + 1) % count) for i in...]
    reshape x4 -> x0, local copies, waits for them, and re-layouts: 12.9 us -> none  [the longest x1 3.93 us: shards(): jnp.broadcast_to(correction[:, :, None, :, None], shape_c)]
  transfers between devices with their start and end apart: 46 -> 0, of which waited for: 14 -> 0; matrix products, arithmetic and copies ran while one was open for 16% -> 0% of each run, Pallas kernels for 0% -> 0%
where the time goes in v1:
time: 51.4 us; the launch traced here: 51.1 us
  Pallas kernels  44.4 us (86%)
  local copies, waits for them, and re-layouts  6.01 us (12%)
  between operations  0.65 us (1%)
    pallas_call x1, Pallas kernels, shards(): pl.pallas_call(functools.partial(kernel, (nrow, ncol, reach_r, reach_c)),...  44.4 us
    unnamed x12, local copies, waits for them, and re-layouts  6.01 us

profile of v1, /device:TPU:0, one launch (start us, length us, event | category | flops | bytes accessed | tf_op | source)
XLA Modules:
  0.0 51.1 jit_solution(6453916573663175574)
XLA Ops:
  0.6 0.0 copy-start
  0.6 1.0 %copy-done = f32[16,64,128]{2,1,0:T(8,128)S(1)} copy-done((f32[16,64,128]{2,1,0:T(8,128)S(1)}, f32[16,64,128]{2,1,0:T(8,128)}, u32[]{:S(2)}) %copy-start) | copy-done | bytes 524312
  1.7 0.0 copy-start.1
  1.7 1.0 %copy-done.1 = f32[16,64,128]{2,1,0:T(8,128)S(1)} copy-done((f32[16,64,128]{2,1,0:T(8,128)S(1)}, f32[16,64,128]{2,1,0:T(8,128)}, u32[]{:S(2)}) %copy-start.1) | copy-done | bytes 524312
  2.7 0.0 copy-start.2
  2.7 1.0 %copy-done.2 = s32[16,64,128]{2,1,0:T(8,128)S(1)} copy-done((s32[16,64,128]{2,1,0:T(8,128)S(1)}, s32[16,64,128]{2,1,0:T(8,128)}, u32[]{:S(2)}) %copy-start.2) | copy-done | bytes 524312
  3.8 0.0 copy-start.3
  3.8 0.7 %copy-done.3 = f32[8]{0:T(128)S(1)} copy-done((f32[8]{0:T(128)S(1)}, f32[8]{0:T(128)}, u32[]{:S(2)}) %copy-start.3) | copy-done | bytes 56
  4.4 0.0 copy-start.4
  4.4 0.7 %copy-done.4 = f32[8]{0:T(128)S(1)} copy-done((f32[8]{0:T(128)S(1)}, f32[8]{0:T(128)}, u32[]{:S(2)}) %copy-start.4) | copy-done | bytes 56
  5.1 44.4 %shard_map.68 = (f32[16,64,128]{2,1,0:T(8,128)S(1)}, f32[16,64,128]{2,1,0:T(8,128)S(1)}) custom-call(f32[8]{0:T(128)S(1)} %copy-done.3, f32[8]{0:T(128)S(1)} %copy-done.4, f32[16,64,128]{2,1,0:T(8,128)S(1)} %copy-done, f32[16,64,128]{2,1,0:T(8,128)S(1)} %copy-done.1, s32[16,64,128]{2,1,0:T(8,128)S(1)} %copy-done.2), custom_call_target="tpu_custom_call" | custom-call | tf_op jit(solution)/shard_map/pallas_call | solution.py:431
  49.5 0.8 %copy.9 = f32[16,64,128]{2,1,0:T(8,128)} copy(f32[16,64,128]{2,1,0:T(8,128)S(1)} %get-tuple-element.4) | data formatting | bytes 1048576
  50.3 0.8 %copy.10 = f32[16,64,128]{2,1,0:T(8,128)} copy(f32[16,64,128]{2,1,0:T(8,128)S(1)} %get-tuple-element.5) | data formatting | bytes 1048576
Async XLA Ops:
  0.6 1.0 %copy-start = (f32[16,64,128]{2,1,0:T(8,128)S(1)}, f32[16,64,128]{2,1,0:T(8,128)}, u32[]{:S(2)}) copy-start(f32[16,64,128]{2,1,0:T(8,128)} %rhs_ref.1) | copy-start | bytes 1572868
  1.7 1.0 %copy-start.1 = (f32[16,64,128]{2,1,0:T(8,128)S(1)}, f32[16,64,128]{2,1,0:T(8,128)}, u32[]{:S(2)}) copy-start(f32[16,64,128]{2,1,0:T(8,128)} %guess_ref.1) | copy-start | bytes 1572868
  2.7 1.0 %copy-start.2 = (s32[16,64,128]{2,1,0:T(8,128)S(1)}, s32[16,64,128]{2,1,0:T(8,128)}, u32[]{:S(2)}) copy-start(s32[16,64,128]{2,1,0:T(8,128)} %mat_ref.1) | copy-start | bytes 1572868
  3.8 0.7 %copy-start.3 = (f32[8]{0:T(128)S(1)}, f32[8]{0:T(128)}, u32[]{:S(2)}) copy-start(f32[8]{0:T(128)} %cond_ref.1) | copy-start | bytes 100
  4.4 0.7 %copy-start.4 = (f32[8]{0:T(128)S(1)}, f32[8]{0:T(128)}, u32[]{:S(2)}) copy-start(f32[8]{0:T(128)} %capa_ref.1) | copy-start | bytes 100

commit v2 on v1

--- a/solution.py
+++ b/solution.py
@@ -29,13 +29,14 @@
 
 def kernel(
     sizes,
-    cond_ref, capa_ref, rhs_ref, guess_ref, mat_ref,
+    cond_in, capa_in, rhs_in, guess_in, mat_in,
     out_ref, res_ref,
+    cond_ref, capa_ref, rhs_ref, guess_ref, mat_ref, isem,
     va, vb, kap, cap, cz, cx, cy, rx, wgt, dia,
-    mhalo, pack_l, pack_r, recv_l, recv_r, kl, kr,
+    uhalo, upack_l, upack_r, ur_l, ur_r, mhalo, pack_l, pack_r, recv_l, recv_r, kl, kr,
     xsum, tile_k, tile_r, grid_k, grid_r,
     hx, hy, hup, hinv, hgain, hback, hres, ecor,
-    fsend, frecv, ksend, krecv, rsend, rrecv,
+    fsend, frecv, usend, urecv, ksend, krecv, rsend, rrecv,
 ):
     nrow, ncol, reach_r, reach_c = sizes
     depth, wx, wy = rhs_ref.shape
@@ -61,6 +62,18 @@
         if (dr, dc) != (0, 0)
     ]
 
+    local = [
+        pltpu.make_async_copy(src, dst, isem.at[index])
+        for index, (src, dst) in enumerate((
+            (guess_in, guess_ref), (rhs_in, rhs_ref), (mat_in, mat_ref),
+            (cond_in, cond_ref), (capa_in, capa_ref),
+        ))
+    ]
+    for copy in local:
+        copy.start()
+    uhalo[...] = jnp.zeros_like(uhalo)
+    ur_l[...] = jnp.zeros_like(ur_l)
+    ur_r[...] = jnp.zeros_like(ur_r)
     grid_k[...] = jnp.zeros_like(grid_k)
     grid_r[...] = jnp.zeros_like(grid_r)
     mhalo[...] = jnp.zeros_like(mhalo)
@@ -79,14 +92,21 @@
             pl.semaphore_signal(barrier, inc=1, device_id=device(dr, dc), device_id_type=MESH)
 
     lane = lane_ids((wx, LANES))
-    for index, source in enumerate((guess_ref, rhs_ref, mat_ref)):
+
+    def packed(plane_of):
         left = jnp.zeros((wx, LANES), jnp.float32)
         right = jnp.zeros((wx, LANES), jnp.float32)
         for z in range(depth):
-            plane = source[z].astype(jnp.float32)
+            plane = plane_of(z)
             here = lane // 8 == z
             left = jnp.where(here, pltpu.roll(plane, (8 * z) % LANES, 1), left)
             right = jnp.where(here, pltpu.roll(plane, (8 * z + 8) % LANES, 1), right)
+        return left, right
+
+    for copy in local:
+        copy.wait()
+    for index, source in enumerate((guess_ref, rhs_ref, mat_ref)):
+        left, right = packed(lambda z: source[z].astype(jnp.float32))
         pack_l[index] = left
         pack_r[index] = right
 
@@ -95,24 +115,53 @@
     pl.semaphore_wait(barrier, tall_p * wide_p - 1)
 
     zs = slice(1, depth + 1)
-    last = slice(wx - HALO, wx)
-    first = slice(0, HALO)
+
+    def edge(dr, width):
+        if dr == 1:
+            return slice(wx - width, wx), slice(HALO - width, HALO)
+        return slice(0, width), slice(HALO + wx, HALO + wx + width)
+
+    def remote(plan, sends, recvs):
+        copies = []
+        for index, (dr, dc, src, dst) in enumerate(plan):
+            copy = pltpu.make_async_remote_copy(
+                src_ref=src, dst_ref=dst, send_sem=sends.at[index], recv_sem=recvs.at[index],
+                device_id=device(dr, dc), device_id_type=MESH,
+            )
+            copies.append((dr, dc, copy))
+        return copies
+
+    def strips(packs, recvs, middle, wide_of):
+        plan = []
+        for dc, pack, recv in ((1, packs[1], recvs[0]), (-1, packs[0], recvs[1])):
+            plan.append((0, dc, pack, recv.at[middle + (own,)]))
+            for dr in (1, -1):
+                src, dst = edge(dr, wide_of)
+                plan.append((dr, dc, pack.at[middle + (src,)], recv.at[middle + (dst,)]))
+        return plan
+
+    near = PRE + 1
     plan = []
-    for dr, src, dst in ((1, last, lo), (-1, first, hi)):
+    for dr in (1, -1):
+        src, dst = edge(dr, near)
+        thin_src, thin_dst = edge(dr, near - 1)
+        shift = 0 if dr == 1 else HALO + wx
+        in_halo = slice(dst.start - shift, dst.stop - shift)
         plan.append((dr, 0, guess_ref.at[:, src, :], va.at[zs, dst, 0:wy]))
-        plan.append((dr, 0, rhs_ref.at[:, src, :], rx.at[:, dst, 0:wy]))
-        plan.append((dr, 0, mat_ref.at[:, src, :], mhalo.at[0 if dr == 1 else 1]))
-    for dc, pack, recv in ((1, pack_r, recv_l), (-1, pack_l, recv_r)):
-        plan.append((0, dc, pack, recv.at[:, own, :]))
-        plan.append((1, dc, pack.at[:, last, :], recv.at[:, lo, :]))
-        plan.append((-1, dc, pack.at[:, first, :], recv.at[:, hi, :]))
-    fine = []
-    for index, (dr, dc, src, dst) in enumerate(plan):
-        copy = pltpu.make_async_remote_copy(
-            src_ref=src, dst_ref=dst, send_sem=fsend.at[index], recv_sem=frecv.at[index],
-            device_id=device(dr, dc), device_id_type=MESH,
-        )
-        fine.append((dr, dc, copy))
+        plan.append((dr, 0, mat_ref.at[:, src, :], mhalo.at[0 if dr == 1 else 1, :, in_halo, :]))
+        plan.append((dr, 0, rhs_ref.at[:, thin_src, :], rx.at[:, thin_dst, 0:wy]))
+    plan += strips((pack_l, pack_r), (recv_l, recv_r), (slice(None),), near)
+    fine = remote(plan, fsend, frecv)
+    plan = []
+    for dr in (1, -1):
+        src, dst = edge(dr, POST + 1)
+        shift = 0 if dr == 1 else HALO + wx
+        src = slice(src.start + HALO, src.stop + HALO)
+        in_halo = slice(dst.start - shift, dst.stop - shift)
+        held = va if PRE % 2 == 0 else vb
+        plan.append((dr, 0, held.at[zs, src, 0:wy], uhalo.at[0 if dr == 1 else 1, :, in_halo, :]))
+    plan += strips((upack_l, upack_r), (ur_l, ur_r), (), POST + 1)
+    pre_edges = remote(plan, usend, urecv)
 
     def start_all(copies):
         for dr, dc, copy in copies:
@@ -207,19 +256,22 @@
         keep[1] = jnp.where(ok, cval, 0.0)
     elane = lane_ids((ext, LANES))
     rim = slice(wy, wy + LANES)
+
+    def unpack(lvals, rvals, dst, first_z):
+        for z in range(depth):
+            shift = (LANES - 8 * z) % LANES
+            a = pltpu.roll(rvals, shift, 1) if shift else rvals
+            shift = (LANES - 8 - 8 * z) % LANES
+            b = pltpu.roll(lvals, shift, 1) if shift else lvals
+            dst[z + first_z, :, rim] = jnp.where(elane < 8, a, jnp.where(elane >= LANES - 8, b, 0.0))
+
     for left, right, dst, first_z in (
         (kl.at[0], kr.at[0], kap, 1),
         (kl.at[1], kr.at[1], cap, 0),
         (recv_l.at[0], recv_r.at[0], va, 1),
         (recv_l.at[1], recv_r.at[1], rx, 0),
     ):
-        lvals, rvals = left[...], right[...]
-        for z in range(depth):
-            shift = (LANES - 8 * z) % LANES
-            a = pltpu.roll(rvals, shift, 1) if shift else rvals
-            shift = (LANES - 8 - 8 * z) % LANES
-            b = pltpu.roll(lvals, shift, 1) if shift else lvals
-            dst[z + first_z, :, rim] = jnp.where(elane < 8, a, jnp.where(elane >= LANES - 8, b, 0.0))
+        unpack(left[...], right[...], dst, first_z)
     zero = jnp.zeros((ext, wy + LANES), jnp.float32)
     for field in (va, vb, kap):
         field[0] = zero
@@ -303,6 +355,8 @@
     spread_r = spread(tile_r, grid_r, rsend, rrecv)
     start_all(spread_r)
     grid_r[0, reach_c, mid, :] = tile_r[0]
+    upack_l[...], upack_r[...] = packed(lambda z: bufs[0][z + 1, own, 0:wy])
+    start_all(pre_edges)
 
     recv_all(spread_k)
     rows_w = grid_r.shape[2]
@@ -378,6 +432,11 @@
 
     lax.fori_loop(0, CSWEEPS, coarse_sweep, 0)
 
+    recv_all(pre_edges)
+    sent_all(pre_edges)
+    bufs[0][zs, lo, 0:wy] = uhalo[0]
+    bufs[0][zs, hi, 0:wy] = uhalo[1]
+    unpack(ur_l[...], ur_r[...], bufs[0], 1)
     own_r = cells_x * reach_r
     low_r = (own_r - 1) // 8 * 8
     top_r = -(-(own_r + cells_x + 1) // 8) * 8
@@ -426,16 +485,22 @@
     coarse = pltpu.VMEM((depth, rows_w, LANES), f32)
     dma = pltpu.SemaphoreType.DMA
     vmem = pl.BlockSpec(memory_space=pltpu.VMEM)
-    smem = pl.BlockSpec(memory_space=pltpu.SMEM)
+    anywhere = pl.BlockSpec(memory_space=pltpu.HBM)
     shape = jax.ShapeDtypeStruct(right_side.shape, f32)
     return pl.pallas_call(
         functools.partial(kernel, (nrow, ncol, reach_r, reach_c)),
         out_shape=(shape, shape),
-        in_specs=[smem, smem, vmem, vmem, vmem],
+        in_specs=[anywhere] * 5,
         out_specs=(vmem, vmem),
         scratch_shapes=[
+            pltpu.SMEM(conductivity.shape, f32), pltpu.SMEM(capacity.shape, f32),
+            pltpu.VMEM(right_side.shape, f32), pltpu.VMEM(guess.shape, f32),
+            pltpu.VMEM(material.shape, jnp.int32), dma((5,)),
             full(depth + 2), full(depth + 2), full(depth + 2), full(depth), full(depth + 1),
             full(depth), full(depth), full(depth), full(depth), full(depth),
+            pltpu.VMEM((2, depth, HALO, wy), f32),
+            pltpu.VMEM((wx, LANES), f32), pltpu.VMEM((wx, LANES), f32),
+            pltpu.VMEM((ext, LANES), f32), pltpu.VMEM((ext, LANES), f32),
             pltpu.VMEM((2, depth, HALO, wy), jnp.int32),
             pltpu.VMEM((3, wx, LANES), f32), pltpu.VMEM((3, wx, LANES), f32),
             pltpu.VMEM((3, ext, LANES), f32), pltpu.VMEM((3, ext, LANES), f32),
@@ -445,7 +510,7 @@
             pltpu.VMEM((2, 2 * reach_c + 1, rows_w, LANES), f32),
             pltpu.VMEM((1, 2 * reach_c + 1, rows_w, LANES), f32),
             coarse, coarse, coarse, coarse, coarse, coarse, coarse, coarse,
-            dma((12,)), dma((12,)),
+            dma((12,)), dma((12,)), dma((8,)), dma((8,)),
             dma((npeers,)), dma((npeers,)), dma((npeers,)), dma((npeers,)),
         ],
         compiler_params=pltpu.CompilerParams(

time: 51.4 us -> 45.5 us (0.89)
  Pallas kernels: 44.4 us -> 38.6 us
    pallas_call x1, Pallas kernels: 44.4 us -> 38.6 us  [shards(): pl.pallas_call(functools.partial(kernel, (nrow, ncol, reach_r, reach_c)),...]
where the time goes in v2:
time: 45.5 us; the launch traced here: 45.2 us
  Pallas kernels  38.6 us (85%)
  local copies, waits for them, and re-layouts  6.01 us (13%)
  between operations  0.65 us (1%)
    pallas_call x1, Pallas kernels, shards(): pl.pallas_call(functools.partial(kernel, (nrow, ncol, reach_r, reach_c)),...  38.6 us
    unnamed x12, local copies, waits for them, and re-layouts  6.01 us

profile of v2, /device:TPU:0, one launch (start us, length us, event | category | flops | bytes accessed | tf_op | source)
XLA Modules:
  0.0 45.2 jit_solution(10025959576651766257)
XLA Ops:
  0.6 0.0 copy-start
  0.6 1.0 %copy-done = f32[16,64,128]{2,1,0:T(8,128)S(1)} copy-done((f32[16,64,128]{2,1,0:T(8,128)S(1)}, f32[16,64,128]{2,1,0:T(8,128)}, u32[]{:S(2)}) %copy-start) | copy-done | bytes 524312
  1.7 0.0 copy-start.1
  1.7 1.0 %copy-done.1 = f32[16,64,128]{2,1,0:T(8,128)S(1)} copy-done((f32[16,64,128]{2,1,0:T(8,128)S(1)}, f32[16,64,128]{2,1,0:T(8,128)}, u32[]{:S(2)}) %copy-start.1) | copy-done | bytes 524312
  2.7 0.0 copy-start.2
  2.7 1.0 %copy-done.2 = s32[16,64,128]{2,1,0:T(8,128)S(1)} copy-done((s32[16,64,128]{2,1,0:T(8,128)S(1)}, s32[16,64,128]{2,1,0:T(8,128)}, u32[]{:S(2)}) %copy-start.2) | copy-done | bytes 524312
  3.8 0.0 copy-start.3
  3.8 0.7 %copy-done.3 = f32[8]{0:T(128)S(1)} copy-done((f32[8]{0:T(128)S(1)}, f32[8]{0:T(128)}, u32[]{:S(2)}) %copy-start.3) | copy-done | bytes 56
  4.4 0.0 copy-start.4
  4.4 0.7 %copy-done.4 = f32[8]{0:T(128)S(1)} copy-done((f32[8]{0:T(128)S(1)}, f32[8]{0:T(128)}, u32[]{:S(2)}) %copy-start.4) | copy-done | bytes 56
  5.1 38.6 %shard_map.68 = (f32[16,64,128]{2,1,0:T(8,128)S(1)}, f32[16,64,128]{2,1,0:T(8,128)S(1)}) custom-call(f32[8]{0:T(128)S(1)} %copy-done.3, f32[8]{0:T(128)S(1)} %copy-done.4, f32[16,64,128]{2,1,0:T(8,128)S(1)} %copy-done, f32[16,64,128]{2,1,0:T(8,128)S(1)} %copy-done.1, s32[16,64,128]{2,1,0:T(8,128)S(1)} %copy-done.2), custom_call_target="tpu_custom_call" | custom-call | tf_op jit(solution)/shard_map/pallas_call | solution.py:490
  43.6 0.8 %copy.9 = f32[16,64,128]{2,1,0:T(8,128)} copy(f32[16,64,128]{2,1,0:T(8,128)S(1)} %get-tuple-element.4) | data formatting | bytes 1048576
  44.4 0.8 %copy.10 = f32[16,64,128]{2,1,0:T(8,128)} copy(f32[16,64,128]{2,1,0:T(8,128)S(1)} %get-tuple-element.5) | data formatting | bytes 1048576
Async XLA Ops:
  0.6 1.0 %copy-start = (f32[16,64,128]{2,1,0:T(8,128)S(1)}, f32[16,64,128]{2,1,0:T(8,128)}, u32[]{:S(2)}) copy-start(f32[16,64,128]{2,1,0:T(8,128)} %rhs_in.1) | copy-start | bytes 1572868
  1.7 1.0 %copy-start.1 = (f32[16,64,128]{2,1,0:T(8,128)S(1)}, f32[16,64,128]{2,1,0:T(8,128)}, u32[]{:S(2)}) copy-start(f32[16,64,128]{2,1,0:T(8,128)} %guess_in.1) | copy-start | bytes 1572868
  2.7 1.0 %copy-start.2 = (s32[16,64,128]{2,1,0:T(8,128)S(1)}, s32[16,64,128]{2,1,0:T(8,128)}, u32[]{:S(2)}) copy-start(s32[16,64,128]{2,1,0:T(8,128)} %mat_in.1) | copy-start | bytes 1572868
  3.8 0.7 %copy-start.3 = (f32[8]{0:T(128)S(1)}, f32[8]{0:T(128)}, u32[]{:S(2)}) copy-start(f32[8]{0:T(128)} %cond_in.1) | copy-start | bytes 100
  4.4 0.7 %copy-start.4 = (f32[8]{0:T(128)S(1)}, f32[8]{0:T(128)}, u32[]{:S(2)}) copy-start(f32[8]{0:T(128)} %capa_in.1) | copy-start | bytes 100

commit v3 on v2

--- a/solution.py
+++ b/solution.py
@@ -309,6 +309,7 @@
         d = d + yprev(yc)
         dia[z] = d
         wgt[z] = jnp.where(k > 0.0, OMEGA / d, 0.0)
+        va[z + 1] = jnp.where(k > 0.0, va[z + 1], 0.0)
         return carry
 
     lax.fori_loop(0, depth, coefs, 0)
@@ -322,12 +323,6 @@
         yc = cy[z]
         t = t + yc * ynext(v)
         return t + yprev(yc * v)
-
-    def clean(z, carry):
-        va[z + 1] = jnp.where(kap[z + 1] > 0.0, va[z + 1], 0.0)
-        return carry
-
-    lax.fori_loop(0, depth, clean, 0)
 
     def sweep(src, dst):
         def body(z, carry):
@@ -514,7 +509,7 @@
             dma((npeers,)), dma((npeers,)), dma((npeers,)), dma((npeers,)),
         ],
         compiler_params=pltpu.CompilerParams(
-            collective_id=0, has_side_effects=True, vmem_limit_bytes=48 * 1024 * 1024
+            collective_id=0, has_side_effects=True, vmem_limit_bytes=58 * 1024 * 1024
         ),
     )(conductivity, capacity, right_side, guess, material)
 

time: 45.5 us -> 42.9 us (0.943)
  local copies, waits for them, and re-layouts: 6.01 us -> 2.74 us
  Pallas kernels: 38.6 us -> 39.3 us
    unnamed x12 -> x4, local copies, waits for them, and re-layouts: 6.01 us -> 2.74 us
    pallas_call x1, Pallas kernels: 38.6 us -> 39.3 us  [shards(): pl.pallas_call(functools.partial(kernel, (nrow, ncol, reach_r, reach_c)),...]
where the time goes in v3:
time: 42.9 us; the launch traced here: 42.7 us
  Pallas kernels  39.3 us (92%)
  local copies, waits for them, and re-layouts  2.74 us (6%)
  between operations  0.65 us (2%)
    pallas_call x1, Pallas kernels, shards(): pl.pallas_call(functools.partial(kernel, (nrow, ncol, reach_r, reach_c)),...  39.3 us
    unnamed x4, local copies, waits for them, and re-layouts  2.74 us

profile of v3, /device:TPU:0, one launch (start us, length us, event | category | flops | bytes accessed | tf_op | source)
XLA Modules:
  0.0 42.7 jit_solution(4023918694067270047)
XLA Ops:
  0.6 39.3 %shard_map.68 = (f32[16,64,128]{2,1,0:T(8,128)}, f32[16,64,128]{2,1,0:T(8,128)}) custom-call(f32[8]{0:T(128)} %cond_in.1, f32[8]{0:T(128)} %capa_in.1, f32[16,64,128]{2,1,0:T(8,128)} %rhs_in.1, f32[16,64,128]{2,1,0:T(8,128)} %guess_in.1, s32[16,64,128]{2,1,0:T(8,128)} %mat_in.1), custom_call_target="tpu_custom_call" | custom-call | tf_op jit(solution)/shard_map/pallas_call | solution.py:485
  40.0 0.0 copy-start
  40.0 1.9 %copy.9 = f32[16,64,128]{2,1,0:T(8,128)} copy(f32[16,64,128]{2,1,0:T(8,128)} %get-tuple-element.4) | data formatting | bytes 1048576
  41.9 0.0 copy-done
  41.9 0.8 %copy.10 = f32[16,64,128]{2,1,0:T(8,128)} copy(f32[16,64,128]{2,1,0:T(8,128)S(1)} %copy-done) | data formatting | bytes 1048576
Async XLA Ops:
  40.0 2.0 %copy-start = (f32[16,64,128]{2,1,0:T(8,128)S(1)}, f32[16,64,128]{2,1,0:T(8,128)}, u32[]{:S(2)}) copy-start(f32[16,64,128]{2,1,0:T(8,128)} %get-tuple-element.5) | copy-start | bytes 1572868

commit v4 on v3

--- a/solution.py
+++ b/solution.py
@@ -30,7 +30,8 @@
 def kernel(
     sizes,
     cond_in, capa_in, rhs_in, guess_in, mat_in,
-    out_ref, res_ref,
+    out_hbm, res_hbm,
+    res_ref, osem,
     cond_ref, capa_ref, rhs_ref, guess_ref, mat_ref, isem,
     va, vb, kap, cap, cz, cx, cy, rx, wgt, dia,
     uhalo, upack_l, upack_r, ur_l, ur_r, mhalo, pack_l, pack_r, recv_l, recv_r, kl, kr,
@@ -456,15 +457,24 @@
         sweep(bufs[0], bufs[1])
         bufs.reverse()
 
+    outs = [pltpu.make_async_copy(bufs[0].at[zs, own, 0:wy], out_hbm, osem.at[0])]
+    outs[0].start()
+
     def finish(z, carry):
-        out_ref[z] = bufs[0][z + 1, own, 0:wy]
         res_ref[z] = inner_residual(bufs[0], z)
         return carry
 
-    lax.fori_loop(0, depth, finish, 0)
+    half = depth // 2
+    for index, part in ((1, (0, half)), (2, (half, depth))):
+        lax.fori_loop(part[0], part[1], finish, 0)
+        planes = slice(part[0], part[1])
+        outs.append(pltpu.make_async_copy(res_ref.at[planes], res_hbm.at[planes], osem.at[index]))
+        outs[-1].start()
     sent_all(fine)
     sent_all(spread_k)
     sent_all(spread_r)
+    for copy in outs:
+        copy.wait()
 
 
 def shards(nrow, ncol, right_side, guess, material, conductivity, capacity):
@@ -479,15 +489,15 @@
     full = lambda planes: pltpu.VMEM((planes, ext, wide), f32)
     coarse = pltpu.VMEM((depth, rows_w, LANES), f32)
     dma = pltpu.SemaphoreType.DMA
-    vmem = pl.BlockSpec(memory_space=pltpu.VMEM)
     anywhere = pl.BlockSpec(memory_space=pltpu.HBM)
     shape = jax.ShapeDtypeStruct(right_side.shape, f32)
     return pl.pallas_call(
         functools.partial(kernel, (nrow, ncol, reach_r, reach_c)),
         out_shape=(shape, shape),
         in_specs=[anywhere] * 5,
-        out_specs=(vmem, vmem),
+        out_specs=(anywhere, anywhere),
         scratch_shapes=[
+            pltpu.VMEM(right_side.shape, f32), dma((3,)),
             pltpu.SMEM(conductivity.shape, f32), pltpu.SMEM(capacity.shape, f32),
             pltpu.VMEM(right_side.shape, f32), pltpu.VMEM(guess.shape, f32),
             pltpu.VMEM(material.shape, jnp.int32), dma((5,)),

time: 42.9 us -> 42.4 us (0.988)
    pallas_call x1, Pallas kernels: 39.3 us -> 38.9 us  [shards(): pl.pallas_call(functools.partial(kernel, (nrow, ncol, reach_r, reach_c)),...]
where the time goes in v4:
time: 42.4 us; the launch traced here: 42.3 us
  Pallas kernels  38.9 us (92%)
  local copies, waits for them, and re-layouts  2.74 us (6%)
  between operations  0.65 us (2%)
    pallas_call x1, Pallas kernels, shards(): pl.pallas_call(functools.partial(kernel, (nrow, ncol, reach_r, reach_c)),...  38.9 us
    unnamed x4, local copies, waits for them, and re-layouts  2.74 us

profile of v4, /device:TPU:0, one launch (start us, length us, event | category | flops | bytes accessed | tf_op | source)
XLA Modules:
  0.0 42.3 jit_solution(464238660478792841)
XLA Ops:
  0.6 38.9 %shard_map.68 = (f32[16,64,128]{2,1,0:T(8,128)}, f32[16,64,128]{2,1,0:T(8,128)}) custom-call(f32[8]{0:T(128)} %cond_in.1, f32[8]{0:T(128)} %capa_in.1, f32[16,64,128]{2,1,0:T(8,128)} %rhs_in.1, f32[16,64,128]{2,1,0:T(8,128)} %guess_in.1, s32[16,64,128]{2,1,0:T(8,128)} %mat_in.1), custom_call_target="tpu_custom_call" | custom-call | tf_op jit(solution)/shard_map/pallas_call | solution.py:494
  39.5 0.0 copy-start
  39.5 1.9 %copy.9 = f32[16,64,128]{2,1,0:T(8,128)} copy(f32[16,64,128]{2,1,0:T(8,128)} %get-tuple-element.4) | data formatting | bytes 1048576
  41.5 0.0 copy-done
  41.5 0.8 %copy.10 = f32[16,64,128]{2,1,0:T(8,128)} copy(f32[16,64,128]{2,1,0:T(8,128)S(1)} %copy-done) | data formatting | bytes 1048576
Async XLA Ops:
  39.5 2.0 %copy-start = (f32[16,64,128]{2,1,0:T(8,128)S(1)}, f32[16,64,128]{2,1,0:T(8,128)}, u32[]{:S(2)}) copy-start(f32[16,64,128]{2,1,0:T(8,128)} %get-tuple-element.5) | copy-start | bytes 1572868
